TPU v7x, 512 devices: a whole 4x8x8 slice. The times are simulated.
512 devices in a mesh: depth: 8 (over y), tile: 64 (over x, z, core).
Axes of the slice: x: 4, y: 8, z: 8, core: 2. Of those that a mesh axis runs over, the one named last changes fastest.
Arguments:
- transmission: float32 [8, 64, 2, 256, 256], P('depth', 'tile'), may hold values from -0.6 to 1.6, as said below
- probe_modes: float32 [4, 2, 128, 128], replicated, may hold values from -3 to 3
- propagator_phase: float32 [128, 128], replicated, may hold values from -3.140625 to 3.140625
- measured: float32 [64, 4, 128, 128], P('tile'), may hold values from 0 to 2
- counts: int32 [64], P('tile'), may hold values from 2 to 4, as said below
- offsets: int32 [64, 4, 2], P('tile'), may hold values from 0 to 384, as said below
Outputs:
- object_grad: float32 [8, 64, 2, 256, 256], P('depth', 'tile')
Inputs may be any that keep to these rules, and one draw needn't show every extreme that they name: `counts`: each tile has 2 to 4 positions, in its first slots; some tile has exactly 4. `offsets`: rows run up to 384, columns up to 384. In every tile, slot 0's patch reaches into the upper and left margins and slot 1's into the lower and right margins. `transmission`: real parts lie near 1 and imaginary parts near 0.
All inputs are finite; a program needn't handle non-finite values.
Results may differ from a plain program's by a relative error of at most 0.014.
Values may be sent and summed in bfloat16 or wider, within the bound.
A program may use at most 64 MiB of HBM per device.

v0:
```python
import math

import jax
import jax.numpy as jnp
from jax import lax
from jax.sharding import PartitionSpec as P

TCOLS = 4


highest = lax.Precision.HIGHEST


def passed_along(array, axis, by):
    peers = lax.axis_size(axis)
    pairs = [(i, i + by) for i in range(peers) if 0 <= i + by < peers]
    return lax.ppermute(array, axis, pairs)


def dft_pair(probe_side):
    index_row = jnp.arange(probe_side, dtype=jnp.int32)
    product = index_row[:, None] * index_row[None, :] % probe_side
    angle_grid = product.astype(jnp.float32) * (-2.0 * math.pi / probe_side)
    norm_factor = 1.0 / math.sqrt(probe_side)
    return (jnp.cos(angle_grid) * norm_factor, jnp.sin(angle_grid) * norm_factor)


def transform(wave_field, pair_table, inverse):
    real_t = pair_table[0]
    imag_t = -pair_table[1] if inverse else pair_table[1]
    wave_re = wave_field[:, 0]
    wave_im = wave_field[:, 1]
    left_re = jnp.einsum("jk,bkl->bjl", real_t, wave_re, precision=highest) - jnp.einsum(
        "jk,bkl->bjl", imag_t, wave_im, precision=highest
    )
    left_im = jnp.einsum("jk,bkl->bjl", real_t, wave_im, precision=highest) + jnp.einsum(
        "jk,bkl->bjl", imag_t, wave_re, precision=highest
    )
    out_re = jnp.einsum("bjk,kl->bjl", left_re, real_t, precision=highest) - jnp.einsum(
        "bjk,kl->bjl", left_im, imag_t, precision=highest
    )
    out_im = jnp.einsum("bjk,kl->bjl", left_re, imag_t, precision=highest) + jnp.einsum(
        "bjk,kl->bjl", left_im, real_t, precision=highest
    )
    return jnp.stack([out_re, out_im], axis=1)


def complex_mul(factor_one, factor_two):
    one_re = factor_one[..., 0, :, :]
    one_im = factor_one[..., 1, :, :]
    two_re = factor_two[..., 0, :, :]
    two_im = factor_two[..., 1, :, :]
    return jnp.stack(
        [one_re * two_re - one_im * two_im, one_re * two_im + one_im * two_re], axis=-3
    )


def conj_mul(factor_one, factor_two):
    one_re = factor_one[..., 0, :, :]
    one_im = factor_one[..., 1, :, :]
    two_re = factor_two[..., 0, :, :]
    two_im = factor_two[..., 1, :, :]
    return jnp.stack(
        [one_re * two_re + one_im * two_im, one_im * two_re - one_re * two_im], axis=-3
    )


def propagate(wave_field, kernel, pair_table):
    spectrum = complex_mul(transform(wave_field, pair_table, False), kernel)
    return transform(spectrum, pair_table, True)


def adjoint(wave_field, kernel, pair_table):
    spectrum = conj_mul(transform(wave_field, pair_table, False), kernel)
    return transform(spectrum, pair_table, True)


def neighbour_faces(piece, offset_by):
    return passed_along(piece, "tile", offset_by)


def margin_back(piece, offset_by):
    return passed_along(piece, "tile", offset_by)


def extend_tile(own_tile, probe_side, grid_cols):
    column = lax.axis_index("tile") % grid_cols
    from_above = neighbour_faces(own_tile[:, -probe_side:], grid_cols)
    from_below = neighbour_faces(own_tile[:, :probe_side], -grid_cols)
    tall_tile = jnp.concatenate([from_above, own_tile, from_below], axis=1)
    from_left = neighbour_faces(tall_tile[:, :, -probe_side:], 1)
    from_right = neighbour_faces(tall_tile[:, :, :probe_side], -1)
    from_left = jnp.where(column > 0, from_left, 0.0)
    from_right = jnp.where(column < grid_cols - 1, from_right, 0.0)
    return jnp.concatenate([from_left, tall_tile, from_right], axis=2)


def fold_tile(grad_pad, probe_side, grid_cols, tile_rows, tile_cols):
    column = lax.axis_index("tile") % grid_cols
    from_right = margin_back(grad_pad[:, :, :probe_side], -1)
    from_left = margin_back(grad_pad[:, :, tile_cols + probe_side :], 1)
    from_right = jnp.where(column < grid_cols - 1, from_right, 0.0)
    from_left = jnp.where(column > 0, from_left, 0.0)
    tall_tile = grad_pad[:, :, probe_side : probe_side + tile_cols]
    tall_tile = tall_tile.at[:, :, :probe_side].add(from_left)
    tall_tile = tall_tile.at[:, :, tile_cols - probe_side :].add(from_right)
    from_below = margin_back(tall_tile[:, :probe_side], -grid_cols)
    from_above = margin_back(tall_tile[:, tile_rows + probe_side :], grid_cols)
    interior = tall_tile[:, probe_side : probe_side + tile_rows]
    interior = interior.at[:, :probe_side].add(from_above)
    interior = interior.at[:, tile_rows - probe_side :].add(from_below)
    return interior


def sectioned_grads(patches, probe_modes, measured, valid_slots, kernel, pair_table):
    slot_count, unused_two, probe_side, unused_side = patches.shape
    mode_count = probe_modes.shape[0]
    item_count = slot_count * mode_count
    patch_items = jnp.repeat(patches, mode_count, axis=0)
    probe_items = jnp.tile(probe_modes, (slot_count, 1, 1, 1))
    section_index = lax.axis_index("depth")
    section_count = lax.axis_size("depth")
    last_section = section_count - 1
    groups = item_count // mode_count
    turn_count = section_count + groups - 1
    empty_wave = jnp.zeros((mode_count, 2, probe_side, probe_side), jnp.bfloat16)
    item_shape = (item_count, 2, probe_side, probe_side)

    def forward_turn(turn_index, state_tuple):
        incoming, stored, exit_waves = state_tuple
        group_index = turn_index - section_index
        active = (group_index >= 0) & (group_index < groups)
        first_item = jnp.clip(group_index, 0, groups - 1) * mode_count

        def forward_advance(operands):
            arrived, stored_now, exits_now = operands
            probe_part = lax.dynamic_slice_in_dim(probe_items, first_item, mode_count, 0)
            entering = jnp.where(section_index == 0, probe_part, arrived.astype(jnp.float32))
            screen = lax.dynamic_slice_in_dim(patch_items, first_item, mode_count, 0)
            leaving = propagate(complex_mul(screen, entering), kernel, pair_table)
            stored_now = lax.dynamic_update_slice_in_dim(stored_now, entering, first_item, 0)
            exits_now = lax.dynamic_update_slice_in_dim(exits_now, leaving, first_item, 0)
            return (leaving.astype(jnp.bfloat16), stored_now, exits_now)

        def forward_standby(operands):
            return (empty_wave, operands[1], operands[2])

        outgoing, stored, exit_waves = lax.cond(
            active, forward_advance, forward_standby, (incoming, stored, exit_waves)
        )
        incoming = passed_along(outgoing, "depth", 1)
        return (incoming, stored, exit_waves)

    start_state = (
        empty_wave,
        jnp.zeros(item_shape, jnp.float32),
        jnp.zeros(item_shape, jnp.float32),
    )
    unused_wave, stored, exit_waves = lax.fori_loop(0, turn_count, forward_turn, start_state)

    def far_field(exits_now):
        far = transform(exits_now, pair_table, False)
        grouped = far.reshape(slot_count, mode_count, 2, probe_side, probe_side)
        intensity = jnp.sum(grouped[:, :, 0] ** 2 + grouped[:, :, 1] ** 2, axis=1)
        weight = 4.0 * valid_slots[:, None, None] * (intensity - measured)
        scaled = grouped * weight[:, None, None, :, :]
        return transform(scaled.reshape(item_shape), pair_table, True)

    def no_far_field(exits_now):
        return jnp.zeros_like(exits_now)

    far_grads = lax.cond(section_index == last_section, far_field, no_far_field, exit_waves)

    def backward_turn(turn_index, state_tuple):
        incoming, item_grads = state_tuple
        group_index = turn_index - (last_section - section_index)
        active = (group_index >= 0) & (group_index < groups)
        first_item = jnp.clip(group_index, 0, groups - 1) * mode_count

        def backward_advance(operands):
            arrived, grads_now = operands
            seed_part = lax.dynamic_slice_in_dim(far_grads, first_item, mode_count, 0)
            arriving = jnp.where(
                section_index == last_section, seed_part, arrived.astype(jnp.float32)
            )
            spread = adjoint(arriving, kernel, pair_table)
            screen = lax.dynamic_slice_in_dim(patch_items, first_item, mode_count, 0)
            entering = lax.dynamic_slice_in_dim(stored, first_item, mode_count, 0)
            passing = conj_mul(spread, screen)
            grads_now = lax.dynamic_update_slice_in_dim(
                grads_now, conj_mul(spread, entering), first_item, 0
            )
            return (passing.astype(jnp.bfloat16), grads_now)

        def backward_standby(operands):
            return (empty_wave, operands[1])

        outgoing, item_grads = lax.cond(
            active, backward_advance, backward_standby, (incoming, item_grads)
        )
        incoming = passed_along(outgoing, "depth", -1)
        return (incoming, item_grads)

    unused_back, item_grads = lax.fori_loop(
        0, turn_count, backward_turn, (empty_wave, jnp.zeros(item_shape, jnp.float32))
    )
    return jnp.sum(item_grads.reshape(slot_count, mode_count, 2, probe_side, probe_side), axis=1)


def body(transmission, probe_modes, propagator_phase, measured, counts, offsets):
    probe_side = probe_modes.shape[-1]
    slot_count = offsets.shape[1]
    tile_rows = transmission.shape[3]
    tile_cols = transmission.shape[4]
    pair_table = dft_pair(probe_side)
    kernel = jnp.stack([jnp.cos(propagator_phase), jnp.sin(propagator_phase)])
    own_tile = transmission[0, 0]
    padded = extend_tile(own_tile, probe_side, TCOLS)
    anchor = jnp.zeros((), jnp.int32)
    row_offsets = offsets[0, :, 0]
    col_offsets = offsets[0, :, 1]

    def cut_patch(row_start, col_start):
        return lax.dynamic_slice(
            padded, (anchor, row_start, col_start), (2, probe_side, probe_side)
        )

    patches = jax.vmap(cut_patch)(row_offsets, col_offsets)
    valid_slots = (jnp.arange(slot_count, dtype=jnp.int32) < counts[0]).astype(jnp.float32)
    patch_grad = sectioned_grads(patches, probe_modes, measured[0], valid_slots, kernel, pair_table)
    grad_pad = jnp.zeros(padded.shape, jnp.float32)
    for slot_index in range(slot_count):
        corner = (anchor, row_offsets[slot_index], col_offsets[slot_index])
        window = lax.dynamic_slice(grad_pad, corner, (2, probe_side, probe_side))
        grad_pad = lax.dynamic_update_slice(grad_pad, window + patch_grad[slot_index], corner)
    interior = fold_tile(grad_pad, probe_side, TCOLS, tile_rows, tile_cols)
    return interior[None, None]


def solution(mesh):
    return jax.shard_map(
        body,
        mesh=mesh,
        in_specs=(
            P("depth", "tile", None, None, None),
            P(),
            P(),
            P("tile", None, None, None),
            P("tile"),
            P("tile", None, None),
        ),
        out_specs=P("depth", "tile", None, None, None),
        check_vma=False,
    )
```

profile of v0, /device:TPU:7, one launch (start us, length us, event | category | flops | bytes accessed | tf_op | source)
XLA Modules:
  0.0 707.2 jit_solution(17408168693513182378)
XLA Ops:
  1.1 5.8 collective-permute-start.2
  6.9 7.0 collective-permute-start.3
  18.2 6.7 collective-permute-done.3
  50.5 10.7 %while.45 = (s32[]{:T(128)}, f32[2,512,512]{2,1,0:T(8,128)S(1)}, s32[4,3]{1,0:T(4,128)S(1)}, f32[4,2,128,128]{3,2,1,0:T(8,128)}, s32[]{:T(128)}) while((s32[]{:T(128)}, f32[2,512,512]{2,1,0:T(8,128)S(1)}, s32[4,3]{1,0:T(4,128)S(1)}, f32[4,2,128,128]{3,2,1,0:T(8,128)}, s32[]{:T(128)}) %tuple.226), condition=%wide.while_cond.4, body=%wide.while_body.4.sunk | while | flops 2 | bytes 263785 | solution.py:224
  68.3 246.1 %while.46 = (s32[]{:T(128)}, bf16[4,2,128,128]{3,2,0,1:T(8,128)(2,1)S(1)}, f32[16,2,128,128]{2,3,0,1:T(8,128)}, f32[16,2,128,128]{3,2,0,1:T(8,128)}, s32[]{:T(12...) while((s32[]{:T(128)}, ...), condition=%wide.region_3.4_spmd.clone.clone, body=%wide.region_0.3_spmd.clone.clone.sunk | while | flops 1613168640 | bytes 26214916 | solution.py:159
  72.5 13.9 %conditional.10 = (bf16[4,2,128,128]{3,2,0,1:T(8,128)(2,1)}, f32[16,2,128,128]{2,3,0,1:T(8,128)}, f32[16,2,128,128]{3,2,0,1:T(8,128)}) conditional(s32[]{:T(128)} %convert_element_type.177, (f32[16,2,128,128]{2,3,0,1:T(8,128)}, f32[16,2,128,128]{3,2,0,1:T(8,128)}) %tuple.218, (s32[]{:T(128)}, f32[16,2,128,128]{2,3,0,1:T(8,128)}, s32[]{:T(128)}, ...), branch_computations={%region_1.1_spmd, %region_2.2_spmd.clone} | conditional | flops 1612939264 | bytes 19792060 | solution.py:148
  87.7 6.4 collective-permute-done
  98.2 13.9 %conditional.10 = (bf16[4,2,128,128]{3,2,0,1:T(8,128)(2,1)}, f32[16,2,128,128]{2,3,0,1:T(8,128)}, f32[16,2,128,128]{3,2,0,1:T(8,128)}) conditional(s32[]{:T(128)} %convert_element_type.177, (f32[16,2,128,128]{2,3,0,1:T(8,128)}, f32[16,2,128,128]{3,2,0,1:T(8,128)}) %tuple.218, (s32[]{:T(128)}, f32[16,2,128,128]{2,3,0,1:T(8,128)}, s32[]{:T(128)}, ...), branch_computations={%region_1.1_spmd, %region_2.2_spmd.clone} | conditional | flops 1612939264 | bytes 19792060 | solution.py:148
  112.1 4.0 collective-permute-start
  116.1 5.5 collective-permute-done
  125.9 13.9 %conditional.10 = (bf16[4,2,128,128]{3,2,0,1:T(8,128)(2,1)}, f32[16,2,128,128]{2,3,0,1:T(8,128)}, f32[16,2,128,128]{3,2,0,1:T(8,128)}) conditional(s32[]{:T(128)} %convert_element_type.177, (f32[16,2,128,128]{2,3,0,1:T(8,128)}, f32[16,2,128,128]{3,2,0,1:T(8,128)}) %tuple.218, (s32[]{:T(128)}, f32[16,2,128,128]{2,3,0,1:T(8,128)}, s32[]{:T(128)}, ...), branch_computations={%region_1.1_spmd, %region_2.2_spmd.clone} | conditional | flops 1612939264 | bytes 19792060 | solution.py:148
  139.8 4.0 collective-permute-start
  143.8 4.6 collective-permute-done
  152.6 13.9 %conditional.10 = (bf16[4,2,128,128]{3,2,0,1:T(8,128)(2,1)}, f32[16,2,128,128]{2,3,0,1:T(8,128)}, f32[16,2,128,128]{3,2,0,1:T(8,128)}) conditional(s32[]{:T(128)} %convert_element_type.177, (f32[16,2,128,128]{2,3,0,1:T(8,128)}, f32[16,2,128,128]{3,2,0,1:T(8,128)}) %tuple.218, (s32[]{:T(128)}, f32[16,2,128,128]{2,3,0,1:T(8,128)}, s32[]{:T(128)}, ...), branch_computations={%region_1.1_spmd, %region_2.2_spmd.clone} | conditional | flops 1612939264 | bytes 19792060 | solution.py:148
  166.5 4.0 collective-permute-start
  170.5 3.6 collective-permute-done
  179.0 17.3 %collective-permute-start = (bf16[4,2,128,128]{3,2,0,1:T(8,128)(2,1)}, bf16[4,2,128,128]{3,2,0,1:T(8,128)(2,1)S(1)}, u32[]{:S(2)}, u32[]{:S(2)}) collective-permute-start(bf16[4,2,128,128]{3,2,0,1:T(8,128)(2,1)} %get-tuple-element.1453), channel_id=1, source_target_pairs={{0,64},{64,128},{128,192},{192,256},{256,320},{320,384},{384,448},... | collective-permute-start | bytes 786440 | tf_op jit(solution)/shard_map/while/body/eval_jaxpr/ppermute | solution.py:17
  196.3 3.6 collective-permute-done
  204.8 3.7 collective-permute-start
  208.5 3.6 collective-permute-done
  217.0 16.1 %collective-permute-start = (bf16[4,2,128,128]{3,2,0,1:T(8,128)(2,1)}, bf16[4,2,128,128]{3,2,0,1:T(8,128)(2,1)S(1)}, u32[]{:S(2)}, u32[]{:S(2)}) collective-permute-start(bf16[4,2,128,128]{3,2,0,1:T(8,128)(2,1)} %get-tuple-element.1453), channel_id=1, source_target_pairs={{0,64},{64,128},{128,192},{192,256},{256,320},{320,384},{384,448},... | collective-permute-start | bytes 786440 | tf_op jit(solution)/shard_map/while/body/eval_jaxpr/ppermute | solution.py:17
  241.6 3.7 collective-permute-start
  253.8 17.0 %collective-permute-start = (bf16[4,2,128,128]{3,2,0,1:T(8,128)(2,1)}, bf16[4,2,128,128]{3,2,0,1:T(8,128)(2,1)S(1)}, u32[]{:S(2)}, u32[]{:S(2)}) collective-permute-start(bf16[4,2,128,128]{3,2,0,1:T(8,128)(2,1)} %get-tuple-element.1453), channel_id=1, source_target_pairs={{0,64},{64,128},{128,192},{192,256},{256,320},{320,384},{384,448},... | collective-permute-start | bytes 786440 | tf_op jit(solution)/shard_map/while/body/eval_jaxpr/ppermute | solution.py:17
  279.3 4.9 collective-permute-start
  292.7 18.1 %collective-permute-start = (bf16[4,2,128,128]{3,2,0,1:T(8,128)(2,1)}, bf16[4,2,128,128]{3,2,0,1:T(8,128)(2,1)S(1)}, u32[]{:S(2)}, u32[]{:S(2)}) collective-permute-start(bf16[4,2,128,128]{3,2,0,1:T(8,128)(2,1)} %get-tuple-element.1453), channel_id=1, source_target_pairs={{0,64},{64,128},{128,192},{192,256},{256,320},{320,384},{384,448},... | collective-permute-start | bytes 786440 | tf_op jit(solution)/shard_map/while/body/eval_jaxpr/ppermute | solution.py:17
  317.4 11.5 %conditional.3 = (f32[16,2,128,128]{2,3,0,1:T(8,128)}) conditional(s32[]{:T(128)} %convert_element_type.132, () %tuple.88, (f32[16,2,128,128]{3,2,0,1:T(8,128)}, f32[128,128]{1,0:T(8,128)S(1)}, f32[128,128]{1,0:T(8,128)S(1)}, f32[128,128]{1,0:T(8,128)S(1)}, f32[128,128]{1,0:T(8,128)S(1)}, /*index=5*/f32[4]{0:T(128)S(1)}, ...), branch_computations={%region_4.5_spmd, %region_5.7_spmd.clone} | conditional | flops 6447333376 | bytes 64618552 | solution.py:172
  330.5 309.8 %while.47 = (s32[]{:T(128)}, bf16[4,2,128,128]{3,2,0,1:T(8,128)(2,1)S(1)}, f32[16,2,128,128]{3,2,0,1:T(8,128)}, s32[]{:T(128)}, s32[]{:T(128)}, /*index=5*/f32[1...) while((s32[]{:T(128)}, ...), condition=%wide.region_10.11_spmd.clone.clone, body=%wide.region_7.10_spmd.clone.clone.sunk | while | flops 1613692928 | bytes 22544828 | solution.py:204
  333.9 7.6 %collective-permute-done.1 = bf16[4,2,128,128]{3,2,0,1:T(8,128)(2,1)S(1)} collective-permute-done((bf16[4,2,128,128]{3,2,0,1:T(8,128)(2,1)}, bf16[4,2,128,128]{3,2,0,1:T(8,128)(2,1)S(1)}, u32[]{:S(2)}, u32[]{:S(2)}) %collective-permute-start.1) | collective-permute-done | bytes 262176 | tf_op jit(solution)/shard_map/while/body/eval_jaxpr/ppermute | solution.py:17
  344.9 16.5 %collective-permute-done.1 = bf16[4,2,128,128]{3,2,0,1:T(8,128)(2,1)S(1)} collective-permute-done((bf16[4,2,128,128]{3,2,0,1:T(8,128)(2,1)}, bf16[4,2,128,128]{3,2,0,1:T(8,128)(2,1)S(1)}, u32[]{:S(2)}, u32[]{:S(2)}) %collective-permute-start.1) | collective-permute-done | bytes 262176 | tf_op jit(solution)/shard_map/while/body/eval_jaxpr/ppermute | solution.py:17
  364.8 10.0 %collective-permute-done.1 = bf16[4,2,128,128]{3,2,0,1:T(8,128)(2,1)S(1)} collective-permute-done((bf16[4,2,128,128]{3,2,0,1:T(8,128)(2,1)}, bf16[4,2,128,128]{3,2,0,1:T(8,128)(2,1)S(1)}, u32[]{:S(2)}, u32[]{:S(2)}) %collective-permute-start.1) | collective-permute-done | bytes 262176 | tf_op jit(solution)/shard_map/while/body/eval_jaxpr/ppermute | solution.py:17
  378.3 14.1 %collective-permute-done.1 = bf16[4,2,128,128]{3,2,0,1:T(8,128)(2,1)S(1)} collective-permute-done((bf16[4,2,128,128]{3,2,0,1:T(8,128)(2,1)}, bf16[4,2,128,128]{3,2,0,1:T(8,128)(2,1)S(1)}, u32[]{:S(2)}, u32[]{:S(2)}) %collective-permute-start.1) | collective-permute-done | bytes 262176 | tf_op jit(solution)/shard_map/while/body/eval_jaxpr/ppermute | solution.py:17
  395.7 15.9 %collective-permute-done.1 = bf16[4,2,128,128]{3,2,0,1:T(8,128)(2,1)S(1)} collective-permute-done((bf16[4,2,128,128]{3,2,0,1:T(8,128)(2,1)}, bf16[4,2,128,128]{3,2,0,1:T(8,128)(2,1)S(1)}, u32[]{:S(2)}, u32[]{:S(2)}) %collective-permute-start.1) | collective-permute-done | bytes 262176 | tf_op jit(solution)/shard_map/while/body/eval_jaxpr/ppermute | solution.py:17
  415.1 10.3 %collective-permute-done.1 = bf16[4,2,128,128]{3,2,0,1:T(8,128)(2,1)S(1)} collective-permute-done((bf16[4,2,128,128]{3,2,0,1:T(8,128)(2,1)}, bf16[4,2,128,128]{3,2,0,1:T(8,128)(2,1)S(1)}, u32[]{:S(2)}, u32[]{:S(2)}) %collective-permute-start.1) | collective-permute-done | bytes 262176 | tf_op jit(solution)/shard_map/while/body/eval_jaxpr/ppermute | solution.py:17
  428.8 120.4 %collective-permute-done.1 = bf16[4,2,128,128]{3,2,0,1:T(8,128)(2,1)S(1)} collective-permute-done((bf16[4,2,128,128]{3,2,0,1:T(8,128)(2,1)}, bf16[4,2,128,128]{3,2,0,1:T(8,128)(2,1)S(1)}, u32[]{:S(2)}, u32[]{:S(2)}) %collective-permute-start.1) | collective-permute-done | bytes 262176 | tf_op jit(solution)/shard_map/while/body/eval_jaxpr/ppermute | solution.py:17
  550.5 13.2 %conditional.11 = (bf16[4,2,128,128]{3,2,0,1:T(8,128)(2,1)}, f32[16,2,128,128]{3,2,0,1:T(8,128)}) conditional(s32[]{:T(128)} %convert_element_type.179, f32[16,2,128,128]{3,2,0,1:T(8,128)} %get-tuple-element.1550, (s32[]{:T(128)}, s32[]{:T(128)}, f32[16,2,128,128]{2,3,0,1:T(8,128)}, bf16[4,2,128,128]{3,2,0,1:T(8,128)(2,1)S(1)}, ...), branch_computations={%region_8.8_spmd, %region_9.9_spmd.clone} | conditional | flops 1613463552 | bytes 18743420 | solution.py:198
  565.0 7.3 %collective-permute-done.1 = bf16[4,2,128,128]{3,2,0,1:T(8,128)(2,1)S(1)} collective-permute-done((bf16[4,2,128,128]{3,2,0,1:T(8,128)(2,1)}, bf16[4,2,128,128]{3,2,0,1:T(8,128)(2,1)S(1)}, u32[]{:S(2)}, u32[]{:S(2)}) %collective-permute-start.1) | collective-permute-done | bytes 262176 | tf_op jit(solution)/shard_map/while/body/eval_jaxpr/ppermute | solution.py:17
  573.6 13.2 %conditional.11 = (bf16[4,2,128,128]{3,2,0,1:T(8,128)(2,1)}, f32[16,2,128,128]{3,2,0,1:T(8,128)}) conditional(s32[]{:T(128)} %convert_element_type.179, f32[16,2,128,128]{3,2,0,1:T(8,128)} %get-tuple-element.1550, (s32[]{:T(128)}, s32[]{:T(128)}, f32[16,2,128,128]{2,3,0,1:T(8,128)}, bf16[4,2,128,128]{3,2,0,1:T(8,128)(2,1)S(1)}, ...), branch_computations={%region_8.8_spmd, %region_9.9_spmd.clone} | conditional | flops 1613463552 | bytes 18743420 | solution.py:198
  588.1 7.2 %collective-permute-done.1 = bf16[4,2,128,128]{3,2,0,1:T(8,128)(2,1)S(1)} collective-permute-done((bf16[4,2,128,128]{3,2,0,1:T(8,128)(2,1)}, bf16[4,2,128,128]{3,2,0,1:T(8,128)(2,1)S(1)}, u32[]{:S(2)}, u32[]{:S(2)}) %collective-permute-start.1) | collective-permute-done | bytes 262176 | tf_op jit(solution)/shard_map/while/body/eval_jaxpr/ppermute | solution.py:17
  596.7 13.2 %conditional.11 = (bf16[4,2,128,128]{3,2,0,1:T(8,128)(2,1)}, f32[16,2,128,128]{3,2,0,1:T(8,128)}) conditional(s32[]{:T(128)} %convert_element_type.179, f32[16,2,128,128]{3,2,0,1:T(8,128)} %get-tuple-element.1550, (s32[]{:T(128)}, s32[]{:T(128)}, f32[16,2,128,128]{2,3,0,1:T(8,128)}, bf16[4,2,128,128]{3,2,0,1:T(8,128)(2,1)S(1)}, ...), branch_computations={%region_8.8_spmd, %region_9.9_spmd.clone} | conditional | flops 1613463552 | bytes 18743420 | solution.py:198
  611.2 7.2 %collective-permute-done.1 = bf16[4,2,128,128]{3,2,0,1:T(8,128)(2,1)S(1)} collective-permute-done((bf16[4,2,128,128]{3,2,0,1:T(8,128)(2,1)}, bf16[4,2,128,128]{3,2,0,1:T(8,128)(2,1)S(1)}, u32[]{:S(2)}, u32[]{:S(2)}) %collective-permute-start.1) | collective-permute-done | bytes 262176 | tf_op jit(solution)/shard_map/while/body/eval_jaxpr/ppermute | solution.py:17
  619.8 13.2 %conditional.11 = (bf16[4,2,128,128]{3,2,0,1:T(8,128)(2,1)}, f32[16,2,128,128]{3,2,0,1:T(8,128)}) conditional(s32[]{:T(128)} %convert_element_type.179, f32[16,2,128,128]{3,2,0,1:T(8,128)} %get-tuple-element.1550, (s32[]{:T(128)}, s32[]{:T(128)}, f32[16,2,128,128]{2,3,0,1:T(8,128)}, bf16[4,2,128,128]{3,2,0,1:T(8,128)(2,1)S(1)}, ...), branch_computations={%region_8.8_spmd, %region_9.9_spmd.clone} | conditional | flops 1613463552 | bytes 18743420 | solution.py:198
  634.3 6.0 collective-permute-done.1
  652.5 23.6 %collective-permute-start.6 = (f32[2,512,128]{2,1,0:T(8,128)S(1)}, f32[2,512,128]{2,1,0:T(8,128)S(1)}, u32[]{:S(2)}, u32[]{:S(2)}) collective-permute-start(f32[2,512,128]{2,1,0:T(8,128)S(1)} %get-tuple-element.1294), channel_id=1, source_target_pairs={{0,1},{1,2},{2,3},{3,4},{4,5},{5,6},{6,7},{7,8},{8,9},{9,10},{10,1... | collective-permute-start | bytes 1572872 | tf_op jit(solution)/shard_map/ppermute | solution.py:17
  678.1 4.1 collective-permute-done.6
  682.3 4.3 collective-permute-done.7
  686.7 4.5 collective-permute-start.8
  691.2 3.8 collective-permute-start.9
  695.1 10.2 %collective-permute-done.8 = f32[2,128,256]{2,1,0:T(8,128)S(1)} collective-permute-done((f32[2,128,256]{2,1,0:T(8,128)S(1)}, f32[2,128,256]{2,1,0:T(8,128)S(1)}, u32[]{:S(2)}, u32[]{:S(2)}) %collective-permute-start.8) | collective-permute-done | bytes 262176 | tf_op jit(solution)/shard_map/ppermute | solution.py:17
  (394 shorter events, 276.7 us)
Async XLA Ops:
  1.1 17.1 %collective-permute-start.2 = (f32[2,128,256]{2,1,0:T(8,128)S(1)}, f32[2,128,256]{2,1,0:T(8,128)S(1)}, u32[]{:S(2)}, u32[]{:S(2)}) collective-permute-start(f32[2,128,256]{2,1,0:T(8,128)S(1)} %get-tuple-element.1299), channel_id=1, source_target_pairs={{0,4},{1,5},{2,6},{3,7},{4,8},{5,9},{6,10},{7,11},{8,12},{9,13},{1... | collective-permute-start | bytes 786440 | tf_op jit(solution)/shard_map/ppermute | solution.py:17
  6.9 18.0 %collective-permute-start.3 = (f32[2,128,256]{2,1,0:T(8,128)S(1)}, f32[2,128,256]{2,1,0:T(8,128)S(1)}, u32[]{:S(2)}, u32[]{:S(2)}) collective-permute-start(f32[2,128,256]{2,1,0:T(8,128)S(1)} %get-tuple-element.1300), channel_id=1, source_target_pairs={{4,0},{5,1},{6,2},{7,3},{8,4},{9,5},{10,6},{11,7},{12,8},{13,9},{1... | collective-permute-start | bytes 786440 | tf_op jit(solution)/shard_map/ppermute | solution.py:17
  17.0 27.0 %copy-start.6 = (f32[4,2,128,128]{3,2,1,0:T(8,128)S(1)}, f32[4,2,128,128]{3,2,1,0:T(8,128)}, u32[]{:S(2)}) copy-start(f32[4,2,128,128]{3,2,1,0:T(8,128)} %param.25) | copy-start | bytes 1572868
  24.8 2.1 copy-start.3
  26.9 23.4 %copy-start.2 = (f32[1,1,2,256,256]{4,3,2,1,0:T(8,128)S(1)}, f32[1,1,2,256,256]{4,3,2,1,0:T(8,128)}, u32[]{:S(2)}) copy-start(f32[1,1,2,256,256]{4,3,2,1,0:T(8,128)} %param.24) | copy-start | bytes 1572868
  26.9 23.3 %collective-permute-start.5 = (f32[2,512,128]{2,1,0:T(8,128)}, f32[2,512,128]{2,1,0:T(8,128)S(1)}, u32[]{:S(2)}, u32[]{:S(2)}) collective-permute-start(f32[2,512,128]{2,1,0:T(8,128)} %get-tuple-element.1298), channel_id=1, source_target_pairs={{1,0},{2,1},{3,2},{4,3},{5,4},{6,5},{7,6},{8,7},{9,8},{10,9},{11,1... | collective-permute-start | bytes 1572872 | tf_op jit(solution)/shard_map/ppermute | solution.py:17
  31.2 19.1 %collective-permute-start.4 = (f32[2,512,128]{2,1,0:T(8,128)S(1)}, f32[2,512,128]{2,1,0:T(8,128)S(1)}, u32[]{:S(2)}, u32[]{:S(2)}) collective-permute-start(f32[2,512,128]{2,1,0:T(8,128)S(1)} %get-tuple-element.1297), channel_id=1, source_target_pairs={{0,1},{1,2},{2,3},{3,4},{4,5},{5,6},{6,7},{7,8},{8,9},{9,10},{10,1... | collective-permute-start | bytes 1572872 | tf_op jit(solution)/shard_map/ppermute | solution.py:17
  49.1 1.3 copy-start.4
  73.6 2.6 copy-start
  73.6 2.6 copy-start.1
  86.4 7.7 %collective-permute-start = (bf16[4,2,128,128]{3,2,0,1:T(8,128)(2,1)}, bf16[4,2,128,128]{3,2,0,1:T(8,128)(2,1)S(1)}, u32[]{:S(2)}, u32[]{:S(2)}) collective-permute-start(bf16[4,2,128,128]{3,2,0,1:T(8,128)(2,1)} %get-tuple-element.1453), channel_id=1, source_target_pairs={{0,64},{64,128},{128,192},{192,256},{256,320},{320,384},{384,448},... | collective-permute-start | bytes 786440 | tf_op jit(solution)/shard_map/while/body/eval_jaxpr/ppermute | solution.py:17
  99.3 2.6 copy-start
  99.3 2.6 copy-start.1
  112.1 9.6 %collective-permute-start = (bf16[4,2,128,128]{3,2,0,1:T(8,128)(2,1)}, bf16[4,2,128,128]{3,2,0,1:T(8,128)(2,1)S(1)}, u32[]{:S(2)}, u32[]{:S(2)}) collective-permute-start(bf16[4,2,128,128]{3,2,0,1:T(8,128)(2,1)} %get-tuple-element.1453), channel_id=1, source_target_pairs={{0,64},{64,128},{128,192},{192,256},{256,320},{320,384},{384,448},... | collective-permute-start | bytes 786440 | tf_op jit(solution)/shard_map/while/body/eval_jaxpr/ppermute | solution.py:17
  127.0 2.6 copy-start
  127.0 2.6 copy-start.1
  139.8 8.6 %collective-permute-start = (bf16[4,2,128,128]{3,2,0,1:T(8,128)(2,1)}, bf16[4,2,128,128]{3,2,0,1:T(8,128)(2,1)S(1)}, u32[]{:S(2)}, u32[]{:S(2)}) collective-permute-start(bf16[4,2,128,128]{3,2,0,1:T(8,128)(2,1)} %get-tuple-element.1453), channel_id=1, source_target_pairs={{0,64},{64,128},{128,192},{192,256},{256,320},{320,384},{384,448},... | collective-permute-start | bytes 786440 | tf_op jit(solution)/shard_map/while/body/eval_jaxpr/ppermute | solution.py:17
  153.6 2.6 copy-start
  153.6 2.6 copy-start.1
  166.5 7.6 %collective-permute-start = (bf16[4,2,128,128]{3,2,0,1:T(8,128)(2,1)}, bf16[4,2,128,128]{3,2,0,1:T(8,128)(2,1)S(1)}, u32[]{:S(2)}, u32[]{:S(2)}) collective-permute-start(bf16[4,2,128,128]{3,2,0,1:T(8,128)(2,1)} %get-tuple-element.1453), channel_id=1, source_target_pairs={{0,64},{64,128},{128,192},{192,256},{256,320},{320,384},{384,448},... | collective-permute-start | bytes 786440 | tf_op jit(solution)/shard_map/while/body/eval_jaxpr/ppermute | solution.py:17
  179.0 20.9 %collective-permute-start = (bf16[4,2,128,128]{3,2,0,1:T(8,128)(2,1)}, bf16[4,2,128,128]{3,2,0,1:T(8,128)(2,1)S(1)}, u32[]{:S(2)}, u32[]{:S(2)}) collective-permute-start(bf16[4,2,128,128]{3,2,0,1:T(8,128)(2,1)} %get-tuple-element.1453), channel_id=1, source_target_pairs={{0,64},{64,128},{128,192},{192,256},{256,320},{320,384},{384,448},... | collective-permute-start | bytes 786440 | tf_op jit(solution)/shard_map/while/body/eval_jaxpr/ppermute | solution.py:17
  204.8 7.3 %collective-permute-start = (bf16[4,2,128,128]{3,2,0,1:T(8,128)(2,1)}, bf16[4,2,128,128]{3,2,0,1:T(8,128)(2,1)S(1)}, u32[]{:S(2)}, u32[]{:S(2)}) collective-permute-start(bf16[4,2,128,128]{3,2,0,1:T(8,128)(2,1)} %get-tuple-element.1453), channel_id=1, source_target_pairs={{0,64},{64,128},{128,192},{192,256},{256,320},{320,384},{384,448},... | collective-permute-start | bytes 786440 | tf_op jit(solution)/shard_map/while/body/eval_jaxpr/ppermute | solution.py:17
  217.0 19.7 %collective-permute-start = (bf16[4,2,128,128]{3,2,0,1:T(8,128)(2,1)}, bf16[4,2,128,128]{3,2,0,1:T(8,128)(2,1)S(1)}, u32[]{:S(2)}, u32[]{:S(2)}) collective-permute-start(bf16[4,2,128,128]{3,2,0,1:T(8,128)(2,1)} %get-tuple-element.1453), channel_id=1, source_target_pairs={{0,64},{64,128},{128,192},{192,256},{256,320},{320,384},{384,448},... | collective-permute-start | bytes 786440 | tf_op jit(solution)/shard_map/while/body/eval_jaxpr/ppermute | solution.py:17
  241.6 7.3 %collective-permute-start = (bf16[4,2,128,128]{3,2,0,1:T(8,128)(2,1)}, bf16[4,2,128,128]{3,2,0,1:T(8,128)(2,1)S(1)}, u32[]{:S(2)}, u32[]{:S(2)}) collective-permute-start(bf16[4,2,128,128]{3,2,0,1:T(8,128)(2,1)} %get-tuple-element.1453), channel_id=1, source_target_pairs={{0,64},{64,128},{128,192},{192,256},{256,320},{320,384},{384,448},... | collective-permute-start | bytes 786440 | tf_op jit(solution)/shard_map/while/body/eval_jaxpr/ppermute | solution.py:17
  253.8 20.6 %collective-permute-start = (bf16[4,2,128,128]{3,2,0,1:T(8,128)(2,1)}, bf16[4,2,128,128]{3,2,0,1:T(8,128)(2,1)S(1)}, u32[]{:S(2)}, u32[]{:S(2)}) collective-permute-start(bf16[4,2,128,128]{3,2,0,1:T(8,128)(2,1)} %get-tuple-element.1453), channel_id=1, source_target_pairs={{0,64},{64,128},{128,192},{192,256},{256,320},{320,384},{384,448},... | collective-permute-start | bytes 786440 | tf_op jit(solution)/shard_map/while/body/eval_jaxpr/ppermute | solution.py:17
  279.3 8.5 %collective-permute-start = (bf16[4,2,128,128]{3,2,0,1:T(8,128)(2,1)}, bf16[4,2,128,128]{3,2,0,1:T(8,128)(2,1)S(1)}, u32[]{:S(2)}, u32[]{:S(2)}) collective-permute-start(bf16[4,2,128,128]{3,2,0,1:T(8,128)(2,1)} %get-tuple-element.1453), channel_id=1, source_target_pairs={{0,64},{64,128},{128,192},{192,256},{256,320},{320,384},{384,448},... | collective-permute-start | bytes 786440 | tf_op jit(solution)/shard_map/while/body/eval_jaxpr/ppermute | solution.py:17
  292.7 21.7 %collective-permute-start = (bf16[4,2,128,128]{3,2,0,1:T(8,128)(2,1)}, bf16[4,2,128,128]{3,2,0,1:T(8,128)(2,1)S(1)}, u32[]{:S(2)}, u32[]{:S(2)}) collective-permute-start(bf16[4,2,128,128]{3,2,0,1:T(8,128)(2,1)} %get-tuple-element.1453), channel_id=1, source_target_pairs={{0,64},{64,128},{128,192},{192,256},{256,320},{320,384},{384,448},... | collective-permute-start | bytes 786440 | tf_op jit(solution)/shard_map/while/body/eval_jaxpr/ppermute | solution.py:17
  314.4 3.0 copy-start.5
  314.4 3.0 copy-start.7
  332.6 8.9 %collective-permute-start.1 = (bf16[4,2,128,128]{3,2,0,1:T(8,128)(2,1)}, bf16[4,2,128,128]{3,2,0,1:T(8,128)(2,1)S(1)}, u32[]{:S(2)}, u32[]{:S(2)}) collective-permute-start(bf16[4,2,128,128]{3,2,0,1:T(8,128)(2,1)} %get-tuple-element.1466), channel_id=1, source_target_pairs={{64,0},{128,64},{192,128},{256,192},{320,256},{384,320},{448,384},... | collective-permute-start | bytes 786440 | tf_op jit(solution)/shard_map/while/body/eval_jaxpr/ppermute | solution.py:17
  343.6 17.8 %collective-permute-start.1 = (bf16[4,2,128,128]{3,2,0,1:T(8,128)(2,1)}, bf16[4,2,128,128]{3,2,0,1:T(8,128)(2,1)S(1)}, u32[]{:S(2)}, u32[]{:S(2)}) collective-permute-start(bf16[4,2,128,128]{3,2,0,1:T(8,128)(2,1)} %get-tuple-element.1466), channel_id=1, source_target_pairs={{64,0},{128,64},{192,128},{256,192},{320,256},{384,320},{448,384},... | collective-permute-start | bytes 786440 | tf_op jit(solution)/shard_map/while/body/eval_jaxpr/ppermute | solution.py:17
  363.5 11.3 %collective-permute-start.1 = (bf16[4,2,128,128]{3,2,0,1:T(8,128)(2,1)}, bf16[4,2,128,128]{3,2,0,1:T(8,128)(2,1)S(1)}, u32[]{:S(2)}, u32[]{:S(2)}) collective-permute-start(bf16[4,2,128,128]{3,2,0,1:T(8,128)(2,1)} %get-tuple-element.1466), channel_id=1, source_target_pairs={{64,0},{128,64},{192,128},{256,192},{320,256},{384,320},{448,384},... | collective-permute-start | bytes 786440 | tf_op jit(solution)/shard_map/while/body/eval_jaxpr/ppermute | solution.py:17
  377.0 15.4 %collective-permute-start.1 = (bf16[4,2,128,128]{3,2,0,1:T(8,128)(2,1)}, bf16[4,2,128,128]{3,2,0,1:T(8,128)(2,1)S(1)}, u32[]{:S(2)}, u32[]{:S(2)}) collective-permute-start(bf16[4,2,128,128]{3,2,0,1:T(8,128)(2,1)} %get-tuple-element.1466), channel_id=1, source_target_pairs={{64,0},{128,64},{192,128},{256,192},{320,256},{384,320},{448,384},... | collective-permute-start | bytes 786440 | tf_op jit(solution)/shard_map/while/body/eval_jaxpr/ppermute | solution.py:17
  394.4 17.2 %collective-permute-start.1 = (bf16[4,2,128,128]{3,2,0,1:T(8,128)(2,1)}, bf16[4,2,128,128]{3,2,0,1:T(8,128)(2,1)S(1)}, u32[]{:S(2)}, u32[]{:S(2)}) collective-permute-start(bf16[4,2,128,128]{3,2,0,1:T(8,128)(2,1)} %get-tuple-element.1466), channel_id=1, source_target_pairs={{64,0},{128,64},{192,128},{256,192},{320,256},{384,320},{448,384},... | collective-permute-start | bytes 786440 | tf_op jit(solution)/shard_map/while/body/eval_jaxpr/ppermute | solution.py:17
  413.8 11.6 %collective-permute-start.1 = (bf16[4,2,128,128]{3,2,0,1:T(8,128)(2,1)}, bf16[4,2,128,128]{3,2,0,1:T(8,128)(2,1)S(1)}, u32[]{:S(2)}, u32[]{:S(2)}) collective-permute-start(bf16[4,2,128,128]{3,2,0,1:T(8,128)(2,1)} %get-tuple-element.1466), channel_id=1, source_target_pairs={{64,0},{128,64},{192,128},{256,192},{320,256},{384,320},{448,384},... | collective-permute-start | bytes 786440 | tf_op jit(solution)/shard_map/while/body/eval_jaxpr/ppermute | solution.py:17
  427.5 121.7 %collective-permute-start.1 = (bf16[4,2,128,128]{3,2,0,1:T(8,128)(2,1)}, bf16[4,2,128,128]{3,2,0,1:T(8,128)(2,1)S(1)}, u32[]{:S(2)}, u32[]{:S(2)}) collective-permute-start(bf16[4,2,128,128]{3,2,0,1:T(8,128)(2,1)} %get-tuple-element.1466), channel_id=1, source_target_pairs={{64,0},{128,64},{192,128},{256,192},{320,256},{384,320},{448,384},... | collective-permute-start | bytes 786440 | tf_op jit(solution)/shard_map/while/body/eval_jaxpr/ppermute | solution.py:17
  563.7 8.6 %collective-permute-start.1 = (bf16[4,2,128,128]{3,2,0,1:T(8,128)(2,1)}, bf16[4,2,128,128]{3,2,0,1:T(8,128)(2,1)S(1)}, u32[]{:S(2)}, u32[]{:S(2)}) collective-permute-start(bf16[4,2,128,128]{3,2,0,1:T(8,128)(2,1)} %get-tuple-element.1466), channel_id=1, source_target_pairs={{64,0},{128,64},{192,128},{256,192},{320,256},{384,320},{448,384},... | collective-permute-start | bytes 786440 | tf_op jit(solution)/shard_map/while/body/eval_jaxpr/ppermute | solution.py:17
  586.8 8.5 %collective-permute-start.1 = (bf16[4,2,128,128]{3,2,0,1:T(8,128)(2,1)}, bf16[4,2,128,128]{3,2,0,1:T(8,128)(2,1)S(1)}, u32[]{:S(2)}, u32[]{:S(2)}) collective-permute-start(bf16[4,2,128,128]{3,2,0,1:T(8,128)(2,1)} %get-tuple-element.1466), channel_id=1, source_target_pairs={{64,0},{128,64},{192,128},{256,192},{320,256},{384,320},{448,384},... | collective-permute-start | bytes 786440 | tf_op jit(solution)/shard_map/while/body/eval_jaxpr/ppermute | solution.py:17
  609.9 8.5 %collective-permute-start.1 = (bf16[4,2,128,128]{3,2,0,1:T(8,128)(2,1)}, bf16[4,2,128,128]{3,2,0,1:T(8,128)(2,1)S(1)}, u32[]{:S(2)}, u32[]{:S(2)}) collective-permute-start(bf16[4,2,128,128]{3,2,0,1:T(8,128)(2,1)} %get-tuple-element.1466), channel_id=1, source_target_pairs={{64,0},{128,64},{192,128},{256,192},{320,256},{384,320},{448,384},... | collective-permute-start | bytes 786440 | tf_op jit(solution)/shard_map/while/body/eval_jaxpr/ppermute | solution.py:17
  633.0 7.3 %collective-permute-start.1 = (bf16[4,2,128,128]{3,2,0,1:T(8,128)(2,1)}, bf16[4,2,128,128]{3,2,0,1:T(8,128)(2,1)S(1)}, u32[]{:S(2)}, u32[]{:S(2)}) collective-permute-start(bf16[4,2,128,128]{3,2,0,1:T(8,128)(2,1)} %get-tuple-element.1466), channel_id=1, source_target_pairs={{64,0},{128,64},{192,128},{256,192},{320,256},{384,320},{448,384},... | collective-permute-start | bytes 786440 | tf_op jit(solution)/shard_map/while/body/eval_jaxpr/ppermute | solution.py:17
  652.5 29.7 %collective-permute-start.6 = (f32[2,512,128]{2,1,0:T(8,128)S(1)}, f32[2,512,128]{2,1,0:T(8,128)S(1)}, u32[]{:S(2)}, u32[]{:S(2)}) collective-permute-start(f32[2,512,128]{2,1,0:T(8,128)S(1)} %get-tuple-element.1294), channel_id=1, source_target_pairs={{0,1},{1,2},{2,3},{3,4},{4,5},{5,6},{6,7},{7,8},{8,9},{9,10},{10,1... | collective-permute-start | bytes 1572872 | tf_op jit(solution)/shard_map/ppermute | solution.py:17
  676.1 10.5 %collective-permute-start.7 = (f32[2,512,128]{2,1,0:T(8,128)S(1)}, f32[2,512,128]{2,1,0:T(8,128)S(1)}, u32[]{:S(2)}, u32[]{:S(2)}) collective-permute-start(f32[2,512,128]{2,1,0:T(8,128)S(1)} %get-tuple-element.1293), channel_id=1, source_target_pairs={{1,0},{2,1},{3,2},{4,3},{5,4},{6,5},{7,6},{8,7},{9,8},{10,9},{11,1... | collective-permute-start | bytes 1572872 | tf_op jit(solution)/shard_map/ppermute | solution.py:17
  686.7 18.5 %collective-permute-start.8 = (f32[2,128,256]{2,1,0:T(8,128)S(1)}, f32[2,128,256]{2,1,0:T(8,128)S(1)}, u32[]{:S(2)}, u32[]{:S(2)}) collective-permute-start(f32[2,128,256]{2,1,0:T(8,128)S(1)} %get-tuple-element.1296), channel_id=1, source_target_pairs={{0,4},{1,5},{2,6},{3,7},{4,8},{5,9},{6,10},{7,11},{8,12},{9,13},{1... | collective-permute-start | bytes 786440 | tf_op jit(solution)/shard_map/ppermute | solution.py:17
  691.2 14.9 %collective-permute-start.9 = (f32[2,128,256]{2,1,0:T(8,128)S(1)}, f32[2,128,256]{2,1,0:T(8,128)S(1)}, u32[]{:S(2)}, u32[]{:S(2)}) collective-permute-start(f32[2,128,256]{2,1,0:T(8,128)S(1)} %get-tuple-element.1295), channel_id=1, source_target_pairs={{4,0},{5,1},{6,2},{7,3},{8,4},{9,5},{10,6},{11,7},{12,8},{13,9},{1... | collective-permute-start | bytes 786440 | tf_op jit(solution)/shard_map/ppermute | solution.py:17
where the time goes:
time: 721 us; the launch traced here: 707 us
  waiting for transfers between devices  294 us (41%)
  starting transfers between devices  161 us (22%)
  local copies, waits for them, and re-layouts  104 us (14%)
  matrix products  73.4 us (10%)
  other arithmetic  45.9 us (6%)
  between operations  16.1 us (2%)
  loops' own time  12.2 us (2%)
    ppermute x30, waiting for transfers between devices, passed_along(): return lax.ppermute(array, axis, pairs)  294 us
    ppermute x30, starting transfers between devices, passed_along(): return lax.ppermute(array, axis, pairs)  161 us
    broadcast_in_dim x22, local copies, waits for them, and re-layouts, sectioned_grads(): patch_items = jnp.repeat(patches, mode_count, axis=0)  42.8 us
    another operation x36, local copies, waits for them, and re-layouts  14.7 us
  transfers between devices with their start and end apart: 30, of which 27 were waited for; matrix products, arithmetic and copies ran while one was open for 1% of the time, Pallas kernels for 0%

commit v1 on v0

v1 whole, which is shorter than its diff:
```python
import functools
import math

import jax
import jax.numpy as jnp
import ml_dtypes
import numpy as np
from jax import lax
from jax.experimental import pallas as pl
from jax.experimental.pallas import tpu as pltpu
from jax.sharding import PartitionSpec as P

TCOLS = 4
N = 128
SCALE = 1.6657
FMODE = 3
BMODE = 1
MESH = pl.DeviceIdType.MESH


def dft_tables():
    k = np.arange(N)
    angle = -2 * np.pi * ((k[:, None] * k[None, :]) % N) / N
    re, im = np.cos(angle) * SCALE, np.sin(angle) * SCALE
    g = np.block([[re, -im], [im, re]])
    both = np.stack([g, g.T]).astype(np.float32)
    high = both.astype(ml_dtypes.bfloat16)
    low = (both - high.astype(np.float32)).astype(ml_dtypes.bfloat16)
    values = np.cos(2 * np.pi * np.arange(N // 4 + 1) / N) * SCALE
    rounded = values.astype(np.float32).astype(ml_dtypes.bfloat16).astype(np.float64)
    gain = float(rounded @ values) / float(values @ values)
    return np.stack([high, low]), gain


TABLES, GAIN = dft_tables()
UNIT = 1.0 / (math.sqrt(N) * SCALE)
UNIT_F = UNIT / GAIN if FMODE == 1 else UNIT
UNIT_B = UNIT / GAIN if BMODE == 1 else UNIT


def blocks(y):
    return y[:N, :N], y[:N, N:], y[N:, :N], y[N:, N:]


def square(a, b, c, d):
    return jnp.concatenate([jnp.concatenate([a, b], 1), jnp.concatenate([c, d], 1)], 0)


def swap(y):
    a, b, c, d = blocks(y)
    return square(a, c, b, d)


def split(x):
    high = x.astype(jnp.bfloat16)
    return high, (x - high.astype(jnp.float32)).astype(jnp.bfloat16)


def dot(a, b):
    return jnp.dot(a, b, preferred_element_type=jnp.float32)


def left(tab, which, x, mode):
    gh = tab[0, which]
    if mode == 1:
        return dot(gh, x.astype(jnp.bfloat16))
    gl = tab[1, which]
    h, l = split(x)
    return dot(jnp.concatenate([gh, gh, gl], 1), jnp.concatenate([h, l, h], 0))


def right(tab, which, x, mode):
    gh = tab[0, which]
    if mode == 1:
        return dot(x.astype(jnp.bfloat16), gh)
    gl = tab[1, which]
    h, l = split(x)
    return dot(jnp.concatenate([h, l, h], 1), jnp.concatenate([gh, gh, gl], 0))


def mul_columns(x, sr, si):
    r1, r2, i1, i2 = blocks(x)
    return square(sr * r1 - si * i1, sr * r2 - si * i2, sr * i1 + si * r1, sr * i2 + si * r2)


def mul_rows(x, sr, si):
    r1, i1, r2, i2 = blocks(x)
    return square(sr * r1 - si * i1, sr * i1 + si * r1, sr * r2 - si * i2, sr * i2 + si * r2)


def propagate(tab, xs, hr, hi, mode):
    xs = [swap(left(tab, 0, x, mode)) for x in xs]
    xs = [mul_rows(right(tab, 1, x, mode), hr, hi) for x in xs]
    xs = [swap(right(tab, 0, x, mode)) for x in xs]
    return [left(tab, 1, x, mode) for x in xs]


def kernel(
    depth, tiles, slots, pairs,
    own, probe, phase, measured, counts, offsets, tab,
    out,
    frame, rows_of, cols_of, rows_back, cols_back, cropped, patch, screens, wave, prop, gout, gin, gcols, gframe,
    hout, hin, vout, vin,
    v_send, v_recv, h_send, h_recv, p_send, p_recv, g_send, g_recv, fh_send, fh_recv, fv_send, fv_recv,
):
    y = lax.axis_index("depth")
    t = lax.axis_index("tile")
    core = lax.rem(t, 2)
    col = lax.rem(t, TCOLS)
    row = lax.div(t, TCOLS)
    has_up, has_down = row > 0, row < tiles // TCOLS - 1
    has_left, has_right = col > 0, col < TCOLS - 1
    bf = jnp.bfloat16
    f32 = jnp.float32

    barrier = pltpu.get_barrier_semaphore()
    around = ((has_up, -TCOLS), (has_down, TCOLS), (has_left, -1), (has_right, 1))
    for there, by in around:
        @pl.when(there)
        def _():
            pl.semaphore_signal(barrier, inc=1, device_id=(y, t + by), device_id_type=MESH)
    for k in range(1, depth):
        pl.semaphore_signal(barrier, inc=1, device_id=(lax.rem(y + k, depth), t), device_id_type=MESH)

    for ri in range(2):
        for cb in range(2):
            frame[ri, 1 + cb, N : 3 * N] = own[ri, :, cb * N : (cb + 1) * N].astype(bf)
    zero = jnp.zeros((2, 2, N, N), bf)

    @pl.when(jnp.logical_not(has_up))
    def _():
        frame[:, 1:3, 0:N] = zero

    @pl.when(jnp.logical_not(has_down))
    def _():
        frame[:, 1:3, 3 * N : 4 * N] = zero

    @pl.when(jnp.logical_not(has_left))
    def _():
        frame[:, 0] = jnp.zeros((2, 4 * N, N), bf)

    @pl.when(jnp.logical_not(has_right))
    def _():
        frame[:, 3] = jnp.zeros((2, 4 * N, N), bf)

    pl.semaphore_wait(
        barrier,
        depth - 1 + sum(there.astype(jnp.int32) for there, _ in around),
    )

    def halo_down():
        return pltpu.make_async_remote_copy(
            src_ref=frame.at[:, 1:3, 2 * N : 3 * N], dst_ref=frame.at[:, 1:3, 0:N],
            send_sem=v_send.at[0], recv_sem=v_recv.at[0], device_id=(y, t + TCOLS), device_id_type=MESH)

    def halo_up():
        return pltpu.make_async_remote_copy(
            src_ref=frame.at[:, 1:3, N : 2 * N], dst_ref=frame.at[:, 1:3, 3 * N : 4 * N],
            send_sem=v_send.at[1], recv_sem=v_recv.at[1], device_id=(y, t - TCOLS), device_id_type=MESH)

    pieces = ((0, N), (3 * N, 4 * N), (N, 3 * N))

    def halo_right(k):
        lo, hi = pieces[k]
        return pltpu.make_async_remote_copy(
            src_ref=frame.at[:, 2, lo:hi], dst_ref=frame.at[:, 0, lo:hi],
            send_sem=h_send.at[0, k], recv_sem=h_recv.at[0, k], device_id=(y, t + 1), device_id_type=MESH)

    def halo_left(k):
        lo, hi = pieces[k]
        return pltpu.make_async_remote_copy(
            src_ref=frame.at[:, 1, lo:hi], dst_ref=frame.at[:, 3, lo:hi],
            send_sem=h_send.at[1, k], recv_sem=h_recv.at[1, k], device_id=(y, t - 1), device_id_type=MESH)

    def sideways(k):
        @pl.when(has_right)
        def _():
            halo_right(k).start()

        @pl.when(has_left)
        def _():
            halo_left(k).start()

    @pl.when(has_down)
    def _():
        halo_down().start()

    @pl.when(has_up)
    def _():
        halo_up().start()

    sideways(2)

    for p in range(slots):
        r, c = offsets[2 * p], offsets[2 * p + 1]
        wide = lax.broadcasted_iota(jnp.int32, (N, 4 * N), 1) - lax.broadcasted_iota(jnp.int32, (N, 4 * N), 0)
        tall = lax.broadcasted_iota(jnp.int32, (4 * N, N), 0) - lax.broadcasted_iota(jnp.int32, (4 * N, N), 1)
        rows_of[p * N : (p + 1) * N] = jnp.where(wide == r, 1.0, 0.0).astype(bf)
        cols_back[p] = jnp.where(wide == c, 1.0, 0.0).astype(bf)
        rows_back[:, p * N : (p + 1) * N] = jnp.where(tall == r, 1.0, 0.0).astype(bf)
        cols_of[p] = jnp.where(tall == c, 1.0, 0.0).astype(bf)
    angle = phase[...]
    prop[0] = jnp.cos(angle)
    prop[1] = jnp.sin(angle)
    for q in range(pairs):
        wave[0, q] = square(probe[2 * q, 0], probe[2 * q + 1, 0], probe[2 * q, 1], probe[2 * q + 1, 1])

    @pl.when(has_up)
    def _():
        halo_down().wait_recv()

    sideways(0)

    @pl.when(has_down)
    def _():
        halo_up().wait_recv()

    sideways(1)

    def crop_rows(cb):
        got = dot(rows_of[...], jnp.concatenate([frame[0, cb], frame[1, cb]], 1)).astype(bf)
        for p in range(slots):
            for ri in range(2):
                cropped[p, ri * N : (ri + 1) * N, cb * N : (cb + 1) * N] = got[p * N : (p + 1) * N, ri * N : (ri + 1) * N]

    crop_rows(1)
    crop_rows(2)
    for k in (2, 0, 1):
        @pl.when(has_left)
        def _():
            halo_right(k).wait_recv()

        @pl.when(has_right)
        def _():
            halo_left(k).wait_recv()

    crop_rows(0)
    crop_rows(3)

    def patch_copy(p, s):
        return pltpu.make_async_remote_copy(
            src_ref=patch.at[p], dst_ref=screens.at[s],
            send_sem=p_send.at[p], recv_sem=p_recv.at[s], device_id=(2 * p + core, t), device_id_type=MESH)

    for p in range(slots):
        got = dot(cropped[p], cols_of[p]).astype(bf)
        patch[p, 0] = got[:N]
        patch[p, 1] = got[N:]

        @pl.when(y != 2 * p + core)
        def _():
            patch_copy(p, y).start()

        @pl.when(y == 2 * p + core)
        def _():
            screens[y] = patch[p]

    mine = lax.div(y, 2)

    def grad_copy(s, p):
        return pltpu.make_async_remote_copy(
            src_ref=gout.at[s], dst_ref=gin.at[p],
            send_sem=g_send.at[s], recv_sem=g_recv.at[p], device_id=(s, t), device_id_type=MESH)

    @pl.when(lax.rem(y, 2) == core)
    def _():
        def screen(s):
            return screens[s, 0].astype(f32), screens[s, 1].astype(f32)

        def arrive(s):
            @pl.when(y != s)
            def _():
                patch_copy(0, s).wait_recv()

        def forward(s, carry):
            arrive(s)
            sr, si = screen(s)
            xs = [mul_columns(wave[s, q], sr, si) for q in range(pairs)]
            xs = propagate(tab, xs, prop[0] * UNIT_F**4, prop[1] * UNIT_F**4, FMODE)
            for q in range(pairs):
                wave[s + 1, q] = xs[q]
            return carry

        lax.fori_loop(0, depth - 1, forward, 0)
        arrive(depth - 1)
        sr, si = screen(depth - 1)
        xs = [mul_columns(wave[depth - 1, q], sr, si) for q in range(pairs)]
        xs = [swap(left(tab, 0, x, FMODE)) for x in xs]
        xs = [mul_rows(right(tab, 1, x, FMODE), prop[0] * UNIT_F**2, prop[1] * UNIT_F**2) for x in xs]
        intensity = jnp.zeros((N, N), f32)
        for x in xs:
            for part in blocks(x):
                intensity = intensity + part * part
        valid = jnp.where(mine < counts[0], 4.0 * UNIT_B**2, 0.0)
        weight = (intensity - measured[mine]) * valid
        xs = [mul_rows(x, prop[0] * weight, -prop[1] * weight) for x in xs]
        xs = [swap(right(tab, 0, x, BMODE)) for x in xs]
        us = [left(tab, 1, x, BMODE) for x in xs]

        def leave(s, us):
            gr = jnp.zeros((N, N), f32)
            gi = jnp.zeros((N, N), f32)
            for q in range(pairs):
                u, v = blocks(us[q]), blocks(wave[s, q])
                for k in range(2):
                    gr = gr + u[k] * v[k] + u[2 + k] * v[2 + k]
                    gi = gi + u[2 + k] * v[k] - u[k] * v[2 + k]
            gout[s, 0] = gr.astype(bf)
            gout[s, 1] = gi.astype(bf)

            @pl.when(y != s)
            def _():
                grad_copy(s, mine).start()

            @pl.when(y == s)
            def _():
                gin[mine] = gout[s]

            sr, si = screen(s)
            for q in range(pairs):
                wave[depth, q] = mul_columns(us[q], sr, -si)

        leave(depth - 1, us)

        def backward(k, carry):
            s = depth - 2 - k
            xs = [wave[depth, q] for q in range(pairs)]
            leave(s, propagate(tab, xs, prop[0] * UNIT_B**4, prop[1] * -(UNIT_B**4), BMODE))
            return carry

        lax.fori_loop(0, depth - 1, backward, 0)

    for p in range(slots):
        @pl.when(y != 2 * p + core)
        def _():
            grad_copy(0, p).wait_recv()

        got = dot(jnp.concatenate([gin[p, 0], gin[p, 1]], 0), cols_back[p]).astype(bf)
        for cb in range(4):
            for ri in range(2):
                gcols[cb, p * N : (p + 1) * N, ri * N : (ri + 1) * N] = got[ri * N : (ri + 1) * N, cb * N : (cb + 1) * N]

    def fold_rows(cb):
        return dot(rows_back[...], gcols[cb])

    def fold_left(k):
        lo, hi = pieces[k]
        return pltpu.make_async_remote_copy(
            src_ref=hout.at[0, :, lo:hi], dst_ref=hin.at[0, :, lo:hi],
            send_sem=fh_send.at[0, k], recv_sem=fh_recv.at[0, k], device_id=(y, t - 1), device_id_type=MESH)

    def fold_right(k):
        lo, hi = pieces[k]
        return pltpu.make_async_remote_copy(
            src_ref=hout.at[1, :, lo:hi], dst_ref=hin.at[1, :, lo:hi],
            send_sem=fh_send.at[1, k], recv_sem=fh_recv.at[1, k], device_id=(y, t + 1), device_id_type=MESH)

    for cb, way in ((0, 0), (3, 1)):
        got = fold_rows(cb).astype(bf)
        hout[way, 0] = got[:, :N]
        hout[way, 1] = got[:, N:]
    for k in range(3):
        @pl.when(has_left)
        def _():
            fold_left(k).start()

        @pl.when(has_right)
        def _():
            fold_right(k).start()

    for cb in (1, 2):
        got = fold_rows(cb)
        gframe[0, cb - 1] = got[:, :N]
        gframe[1, cb - 1] = got[:, N:]

    def fold_up():
        return pltpu.make_async_remote_copy(
            src_ref=vout.at[0], dst_ref=vin.at[0],
            send_sem=fv_send.at[0], recv_sem=fv_recv.at[0], device_id=(y, t - TCOLS), device_id_type=MESH)

    def fold_down():
        return pltpu.make_async_remote_copy(
            src_ref=vout.at[1], dst_ref=vin.at[1],
            send_sem=fv_send.at[1], recv_sem=fv_recv.at[1], device_id=(y, t + TCOLS), device_id_type=MESH)

    def take_sides(k):
        lo, hi = pieces[k]

        @pl.when(has_right)
        def _():
            fold_left(k).wait_recv()
            for ri in range(2):
                gframe[ri, 1, lo:hi] = gframe[ri, 1, lo:hi] + hin[0, ri, lo:hi].astype(f32)

        @pl.when(has_left)
        def _():
            fold_right(k).wait_recv()
            for ri in range(2):
                gframe[ri, 0, lo:hi] = gframe[ri, 0, lo:hi] + hin[1, ri, lo:hi].astype(f32)

    take_sides(0)
    vout[0] = gframe[:, :, 0:N].astype(bf)

    @pl.when(has_up)
    def _():
        fold_up().start()

    take_sides(1)
    vout[1] = gframe[:, :, 3 * N : 4 * N].astype(bf)

    @pl.when(has_down)
    def _():
        fold_down().start()

    take_sides(2)
    for ri in range(2):
        for cb in range(2):
            out[ri, :, cb * N : (cb + 1) * N] = gframe[ri, cb, N : 3 * N]

    @pl.when(has_up)
    def _():
        fold_down().wait_recv()
        for ri in range(2):
            for cb in range(2):
                at = (ri, slice(0, N), slice(cb * N, (cb + 1) * N))
                out[at] = out[at] + vin[1, ri, cb].astype(f32)

    @pl.when(has_down)
    def _():
        fold_up().wait_recv()
        for ri in range(2):
            for cb in range(2):
                at = (ri, slice(N, 2 * N), slice(cb * N, (cb + 1) * N))
                out[at] = out[at] + vin[0, ri, cb].astype(f32)

    @pl.when(has_down)
    def _():
        halo_down().wait_send()
        fold_down().wait_send()

    @pl.when(has_up)
    def _():
        halo_up().wait_send()
        fold_up().wait_send()

    @pl.when(has_right)
    def _():
        for k in range(3):
            halo_right(k).wait_send()
            fold_right(k).wait_send()

    @pl.when(has_left)
    def _():
        for k in range(3):
            halo_left(k).wait_send()
            fold_left(k).wait_send()

    for p in range(slots):
        @pl.when(y != 2 * p + core)
        def _():
            patch_copy(p, 0).wait_send()

    for s in range(depth):
        @pl.when(jnp.logical_and(lax.rem(y, 2) == core, y != s))
        def _():
            grad_copy(s, 0).wait_send()


def body(depth, tiles, transmission, probe_modes, propagator_phase, measured, counts, offsets):
    slots = offsets.shape[1]
    pairs = probe_modes.shape[0] // 2
    bf, f32 = jnp.bfloat16, jnp.float32
    vmem = pl.BlockSpec(memory_space=pltpu.VMEM)
    smem = pl.BlockSpec(memory_space=pltpu.SMEM)
    dma = pltpu.SemaphoreType.DMA
    grad = pl.pallas_call(
        functools.partial(kernel, depth, tiles, slots, pairs),
        out_shape=jax.ShapeDtypeStruct((2, 2 * N, 2 * N), f32),
        in_specs=[vmem, vmem, vmem, vmem, smem, smem, vmem],
        out_specs=vmem,
        scratch_shapes=[
            pltpu.VMEM((2, 4, 4 * N, N), bf),
            pltpu.VMEM((slots * N, 4 * N), bf),
            pltpu.VMEM((slots, 4 * N, N), bf),
            pltpu.VMEM((4 * N, slots * N), bf),
            pltpu.VMEM((slots, N, 4 * N), bf),
            pltpu.VMEM((slots, 2 * N, 4 * N), bf),
            pltpu.VMEM((slots, 2, N, N), bf),
            pltpu.VMEM((depth, 2, N, N), bf),
            pltpu.VMEM((depth + 1, pairs, 2 * N, 2 * N), f32),
            pltpu.VMEM((2, N, N), f32),
            pltpu.VMEM((depth, 2, N, N), bf),
            pltpu.VMEM((slots, 2, N, N), bf),
            pltpu.VMEM((4, slots * N, 2 * N), bf),
            pltpu.VMEM((2, 2, 4 * N, N), f32),
            pltpu.VMEM((2, 2, 4 * N, N), bf),
            pltpu.VMEM((2, 2, 4 * N, N), bf),
            pltpu.VMEM((2, 2, 2, N, N), bf),
            pltpu.VMEM((2, 2, 2, N, N), bf),
            dma((2,)), dma((2,)), dma((2, 3)), dma((2, 3)),
            dma((slots,)), dma((depth,)), dma((depth,)), dma((slots,)),
            dma((2, 3)), dma((2, 3)), dma((2,)), dma((2,)),
        ],
        compiler_params=pltpu.CompilerParams(
            collective_id=0, has_side_effects=True, vmem_limit_bytes=48 * 2**20
        ),
        cost_estimate=pl.CostEstimate(flops=2 * 10**10, bytes_accessed=3 * 2**20, transcendentals=2 * N * N),
    )(
        transmission[0, 0], probe_modes, propagator_phase, measured[0], counts, offsets.reshape(-1),
        jnp.asarray(TABLES),
    )
    return grad[None, None]


def solution(mesh):
    return jax.shard_map(
        functools.partial(body, mesh.shape["depth"], mesh.shape["tile"]),
        mesh=mesh,
        in_specs=(
            P("depth", "tile", None, None, None),
            P(),
            P(),
            P("tile", None, None, None),
            P("tile"),
            P("tile", None, None),
        ),
        out_specs=P("depth", "tile", None, None, None),
        check_vma=False,
    )
```

time: 721 us -> 74.4 us (0.10); the launches traced: 707 us -> 73.5 us
  waiting for transfers between devices: 294 us -> 0 us
  starting transfers between devices: 161 us -> 0 us
  local copies, waits for them, and re-layouts: 104 us -> 6.56 us
  matrix products: 73.4 us -> 0 us
  Pallas kernels: 0 us -> 66.3 us
  other arithmetic: 45.9 us -> 0 us
  between operations: 16.1 us -> 0.68 us
  loops' own time: 12.2 us -> 0 us
    ppermute x30 -> x0, waiting for transfers between devices: 294 us -> none  [passed_along(): return lax.ppermute(array, axis, pairs)]
    ppermute x30 -> x0, starting transfers between devices: 161 us -> none  [passed_along(): return lax.ppermute(array, axis, pairs)]
    dot_general x128 -> x0, matrix products: 73.4 us -> none  [the longest x16 13.7 us: transform(): jnp.einsum('bjk,kl->bjl', left_im, imag_t, precision=highest)]
    pallas_call x0 -> x1, Pallas kernels: none -> 66.3 us  [body(): pl.pallas_call(functools.partial(kernel, depth, tiles, slots, pairs), out...]
    broadcast_in_dim x39 -> x0, local copies, waits for them, and re-layouts: 53.5 us -> none  [the longest x22 42.8 us: sectioned_grads(): patch_items = jnp.repeat(patches, mode_count, axis=0)]
    another operation x48 -> x0, local copies, waits for them, and re-layouts: 18.5 us -> none
    another operation x26 -> x0, loops' own time: 12.2 us -> none  [the longest x1 9.88 us: sectioned_grads(): lax.cond(section_index == last_section, far_field, no_far_field, exit_waves)]
    gather x12 -> x0, local copies, waits for them, and re-layouts: 10.6 us -> none
  transfers between devices with their start and end apart: 30 -> 0, of which waited for: 27 -> 0; matrix products, arithmetic and copies ran while one was open for 1% -> 0% of each run, Pallas kernels for 0% -> 0%
where the time goes in v1:
time: 74.4 us; the launch traced here: 73.5 us
  Pallas kernels  66.3 us (89%)
  local copies, waits for them, and re-layouts  6.56 us (9%)
    pallas_call x1, Pallas kernels, body(): pl.pallas_call(functools.partial(kernel, depth, tiles, slots, pairs), out...  66.3 us
    unnamed x14, local copies, waits for them, and re-layouts  6.47 us

profile of v1, /device:TPU:7, one launch (start us, length us, event | category | flops | bytes accessed | tf_op | source)
XLA Modules:
  0.0 73.5 jit_solution(5056612789534818019)
XLA Ops:
  0.7 0.0 copy-start.5
  0.7 0.7 copy-done.5
  1.3 0.1 copy.9
  1.4 0.1 reshape.3.offsets
  1.5 0.0 copy-start
  1.5 1.0 %copy-done = f32[1,1,2,256,256]{4,3,2,1,0:T(8,128)S(1)} copy-done((f32[1,1,2,256,256]{4,3,2,1,0:T(8,128)S(1)}, f32[1,1,2,256,256]{4,3,2,1,0:T(8,128)}, u32[]{:S(2)}) %copy-start) | copy-done | bytes 524312
  2.6 0.0 copy-start.1
  2.6 1.0 %copy-done.1 = f32[4,2,128,128]{3,2,1,0:T(8,128)S(1)} copy-done((f32[4,2,128,128]{3,2,1,0:T(8,128)S(1)}, f32[4,2,128,128]{3,2,1,0:T(8,128)}, u32[]{:S(2)}) %copy-start.1) | copy-done | bytes 524312
  3.6 0.0 copy-start.2
  3.6 0.9 %copy-done.2 = f32[1,4,128,128]{3,2,1,0:T(8,128)S(1)} copy-done((f32[1,4,128,128]{3,2,1,0:T(8,128)S(1)}, f32[1,4,128,128]{3,2,1,0:T(8,128)}, u32[]{:S(2)}) %copy-start.2) | copy-done | bytes 262168
  4.5 0.0 copy-start.3
  4.5 0.8 %copy-done.3 = f32[128,128]{1,0:T(8,128)S(1)} copy-done((f32[128,128]{1,0:T(8,128)S(1)}, f32[128,128]{1,0:T(8,128)}, u32[]{:S(2)}) %copy-start.3) | copy-done | bytes 65560
  5.4 0.0 copy-start.4
  5.4 1.0 %copy-done.4 = bf16[2,2,256,256]{3,2,1,0:T(8,128)(2,1)S(1)} copy-done((bf16[2,2,256,256]{3,2,1,0:T(8,128)(2,1)S(1)}, bf16[2,2,256,256]{3,2,1,0:T(8,128)(2,1)}, u32[]{:S(2)}) %copy-start.4) | copy-done | bytes 524312
  6.4 66.3 %shard_map.73 = f32[2,256,256]{2,1,0:T(8,128)S(1)} custom-call(f32[2,256,256]{2,1,0:T(8,128)S(1)} %bitcast.4, f32[4,2,128,128]{3,2,1,0:T(8,128)S(1)} %copy-done.1, f32[128,128]{1,0:T(8,128)S(1)} %copy-done.3, f32[4,128,128]{2,1,0:T(8,128)S(1)} %bitcast.5, s32[1]{0:T(128)S(6)} %copy.11.counts, s32[8]{0:T(128)S(1)} %reshape.3.offsets, ...), custom_call_target="tpu_custom_call" | custom-call | flops 20000000000 | bytes 3145728 | tf_op jit(solution)/shard_map/pallas_call | solution.py:476
  72.7 0.8 %copy.12 = f32[1,1,2,256,256]{4,3,2,1,0:T(8,128)} copy(f32[1,1,2,256,256]{4,3,2,1,0:T(8,128)S(1)} %bitcast.3) | data formatting | bytes 1048576
Async XLA Ops:
  0.7 0.7 copy-start.5
  1.5 1.0 %copy-start = (f32[1,1,2,256,256]{4,3,2,1,0:T(8,128)S(1)}, f32[1,1,2,256,256]{4,3,2,1,0:T(8,128)}, u32[]{:S(2)}) copy-start(f32[1,1,2,256,256]{4,3,2,1,0:T(8,128)} %param.7) | copy-start | bytes 1572868
  2.6 1.0 %copy-start.1 = (f32[4,2,128,128]{3,2,1,0:T(8,128)S(1)}, f32[4,2,128,128]{3,2,1,0:T(8,128)}, u32[]{:S(2)}) copy-start(f32[4,2,128,128]{3,2,1,0:T(8,128)} %probe.1) | copy-start | bytes 1572868
  3.6 0.9 %copy-start.2 = (f32[1,4,128,128]{3,2,1,0:T(8,128)S(1)}, f32[1,4,128,128]{3,2,1,0:T(8,128)}, u32[]{:S(2)}) copy-start(f32[1,4,128,128]{3,2,1,0:T(8,128)} %param.10) | copy-start | bytes 786436
  4.5 0.8 %copy-start.3 = (f32[128,128]{1,0:T(8,128)S(1)}, f32[128,128]{1,0:T(8,128)}, u32[]{:S(2)}) copy-start(f32[128,128]{1,0:T(8,128)} %phase.1) | copy-start | bytes 196612
  5.4 1.0 %copy-start.4 = (bf16[2,2,256,256]{3,2,1,0:T(8,128)(2,1)S(1)}, bf16[2,2,256,256]{3,2,1,0:T(8,128)(2,1)}, u32[]{:S(2)}) copy-start(bf16[2,2,256,256]{3,2,1,0:T(8,128)(2,1)} %constant.2.clone.tab) | copy-start | bytes 1572868

commit v2 on v1

v2 whole, which is shorter than its diff:
```python
import functools
import math

import jax
import jax.numpy as jnp
import ml_dtypes
import numpy as np
from jax import lax
from jax.experimental import pallas as pl
from jax.experimental.pallas import tpu as pltpu
from jax.sharding import PartitionSpec as P

TCOLS = 4
N = 128
MESH = pl.DeviceIdType.MESH
CLASS_SCALES = 1.2742026, 1.2925407, 1.5548331, 1.5449858, 1.3945649, 1.3043629, 1.3043644, 1.3043595


def dft_tables():
    k = np.arange(N)
    scale = np.array([CLASS_SCALES[-1 if j == 0 else (j & -j).bit_length() - 1] for j in range(N)])
    angle = -2 * np.pi * ((k[:, None] * k[None, :]) % N) / N
    exact = np.exp(1j * angle)
    held = exact * scale[:, None] * scale[None, :]
    re, im = held.real.astype(np.float32).astype(ml_dtypes.bfloat16), held.imag.astype(np.float32).astype(ml_dtypes.bfloat16)
    rounded = (re.astype(np.float64) + 1j * im.astype(np.float64)) / (scale[:, None] * scale[None, :])
    gain = (rounded * exact.conj()).sum(1).real / N
    g = np.block([[re, -im], [im, re]])
    after = 1 / (scale * gain * math.sqrt(N))
    before = 1 / scale
    outer = [np.outer(v, v) for v in (after * before, after, before, 1 / after)]
    return np.stack([g, g.T]), np.stack(outer).astype(np.float32)


TABLES, FACTORS = dft_tables()


def blocks(y):
    return y[:N, :N], y[:N, N:], y[N:, :N], y[N:, N:]


def square(a, b, c, d):
    return jnp.concatenate([jnp.concatenate([a, b], 1), jnp.concatenate([c, d], 1)], 0)


def swap(y):
    a, b, c, d = blocks(y)
    return square(a, c, b, d)


def dot(a, b):
    return jnp.dot(a, b, preferred_element_type=jnp.float32)


def left(tab, which, x):
    return dot(tab[which], x.astype(jnp.bfloat16))


def right(tab, which, x):
    return dot(x.astype(jnp.bfloat16), tab[which])


def mul_columns(x, sr, si):
    r1, r2, i1, i2 = blocks(x)
    return square(sr * r1 - si * i1, sr * r2 - si * i2, sr * i1 + si * r1, sr * i2 + si * r2)


def mul_rows(x, sr, si):
    r1, i1, r2, i2 = blocks(x)
    return square(sr * r1 - si * i1, sr * i1 + si * r1, sr * r2 - si * i2, sr * i2 + si * r2)


def propagate(tab, xs, hr, hi):
    xs = [swap(left(tab, 0, x)) for x in xs]
    xs = [mul_rows(right(tab, 1, x), hr, hi) for x in xs]
    xs = [swap(right(tab, 0, x)) for x in xs]
    return [left(tab, 1, x) for x in xs]


def kernel(
    depth, tiles, slots, pairs,
    own_hbm, probe_hbm, phase_hbm, measured_hbm, counts, offsets, tab_hbm, fac_hbm,
    out,
    own, probe, phase, measured, tab, fac,
    frame, rows_of, cols_of, rows_back, cols_back, cropped, patch, screens, wave, prop, gout, gin, gcols, gframe,
    hout, hin, vout, vin,
    own_sem, in_sem,
    v_send, v_recv, h_send, h_recv, p_send, p_recv, g_send, g_recv, fh_send, fh_recv, fv_send, fv_recv,
):
    y = lax.axis_index("depth")
    t = lax.axis_index("tile")
    core = lax.rem(t, 2)
    col = lax.rem(t, TCOLS)
    row = lax.div(t, TCOLS)
    has_up, has_down = row > 0, row < tiles // TCOLS - 1
    has_left, has_right = col > 0, col < TCOLS - 1
    bf = jnp.bfloat16
    f32 = jnp.float32

    def load_own(ri, half):
        part = (ri, slice(half * N, (half + 1) * N))
        return pltpu.make_async_copy(own_hbm.at[part], own.at[part], own_sem.at[ri, half])

    def load(k):
        src, dst = ((phase_hbm, phase), (probe_hbm, probe), (tab_hbm, tab), (measured_hbm, measured), (fac_hbm, fac))[k]
        return pltpu.make_async_copy(src, dst, in_sem.at[k])

    for ri in range(2):
        for half in range(2):
            load_own(ri, half).start()

    barrier = pltpu.get_barrier_semaphore()
    around = ((has_up, -TCOLS), (has_down, TCOLS), (has_left, -1), (has_right, 1))
    for there, by in around:
        @pl.when(there)
        def _():
            pl.semaphore_signal(barrier, inc=1, device_id=(y, t + by), device_id_type=MESH)
    for k in range(1, depth):
        pl.semaphore_signal(barrier, inc=1, device_id=(lax.rem(y + k, depth), t), device_id_type=MESH)

    for k in range(5):
        load(k).start()

    def outside(ri, shape):
        return jnp.full(shape, -1.0 if ri == 0 else 0.0, bf)


    @pl.when(jnp.logical_not(has_up))
    def _():
        for ri in range(2):
            frame[ri, 1:3, 0:N] = outside(ri, (2, N, N))

    @pl.when(jnp.logical_not(has_down))
    def _():
        for ri in range(2):
            frame[ri, 1:3, 3 * N : 4 * N] = outside(ri, (2, N, N))

    @pl.when(jnp.logical_not(has_left))
    def _():
        for ri in range(2):
            frame[ri, 0] = outside(ri, (4 * N, N))

    @pl.when(jnp.logical_not(has_right))
    def _():
        for ri in range(2):
            frame[ri, 3] = outside(ri, (4 * N, N))

    for ri in range(2):
        for half in range(2):
            load_own(ri, half).wait()
            for cb in range(2):
                got = own[ri, half * N : (half + 1) * N, cb * N : (cb + 1) * N]
                frame[ri, 1 + cb, (1 + half) * N : (2 + half) * N] = (got - 1.0 if ri == 0 else got).astype(bf)

    pl.semaphore_wait(
        barrier,
        depth - 1 + sum(there.astype(jnp.int32) for there, _ in around),
    )

    def halo_down(ri):
        return pltpu.make_async_remote_copy(
            src_ref=frame.at[ri, 1:3, 2 * N : 3 * N], dst_ref=frame.at[ri, 1:3, 0:N],
            send_sem=v_send.at[0, ri], recv_sem=v_recv.at[0, ri], device_id=(y, t + TCOLS), device_id_type=MESH)

    def halo_up(ri):
        return pltpu.make_async_remote_copy(
            src_ref=frame.at[ri, 1:3, N : 2 * N], dst_ref=frame.at[ri, 1:3, 3 * N : 4 * N],
            send_sem=v_send.at[1, ri], recv_sem=v_recv.at[1, ri], device_id=(y, t - TCOLS), device_id_type=MESH)

    pieces = ((0, N), (3 * N, 4 * N), (N, 3 * N))

    def halo_right(ri, k):
        lo, hi = pieces[k]
        return pltpu.make_async_remote_copy(
            src_ref=frame.at[ri, 2, lo:hi], dst_ref=frame.at[ri, 0, lo:hi],
            send_sem=h_send.at[0, ri, k], recv_sem=h_recv.at[0, ri, k], device_id=(y, t + 1), device_id_type=MESH)

    def halo_left(ri, k):
        lo, hi = pieces[k]
        return pltpu.make_async_remote_copy(
            src_ref=frame.at[ri, 1, lo:hi], dst_ref=frame.at[ri, 3, lo:hi],
            send_sem=h_send.at[1, ri, k], recv_sem=h_recv.at[1, ri, k], device_id=(y, t - 1), device_id_type=MESH)

    def sideways(ri, k):
        @pl.when(has_right)
        def _():
            halo_right(ri, k).start()

        @pl.when(has_left)
        def _():
            halo_left(ri, k).start()

    for ri in range(2):
        @pl.when(has_down)
        def _():
            halo_down(ri).start()

        @pl.when(has_up)
        def _():
            halo_up(ri).start()

    for ri in range(2):
        sideways(ri, 2)

    for p in range(slots):
        r, c = offsets[0, p], offsets[1, p]
        wide = lax.broadcasted_iota(jnp.int32, (N, 4 * N), 1) - lax.broadcasted_iota(jnp.int32, (N, 4 * N), 0)
        tall = lax.broadcasted_iota(jnp.int32, (4 * N, N), 0) - lax.broadcasted_iota(jnp.int32, (4 * N, N), 1)
        rows_of[p * N : (p + 1) * N] = jnp.where(wide == r, 1.0, 0.0).astype(bf)
        cols_back[p] = jnp.where(wide == c, 1.0, 0.0).astype(bf)
        rows_back[:, p * N : (p + 1) * N] = jnp.where(tall == r, 1.0, 0.0).astype(bf)
        cols_of[p] = jnp.where(tall == c, 1.0, 0.0).astype(bf)
    load(0).wait()
    angle = phase[...]
    hr, hi = jnp.cos(angle), jnp.sin(angle)
    load(4).wait()
    prop[0] = hr * fac[0]
    prop[1] = hi * fac[0]
    prop[2] = hr * fac[1]
    prop[3] = hi * fac[1]
    prop[4] = hr * fac[2]
    prop[5] = hi * fac[2]
    load(1).wait()
    for q in range(pairs):
        one, two = probe[2 * q], probe[2 * q + 1]
        wave[0, q] = square(one[0] * fac[3], two[0] * fac[3], one[1] * fac[3], two[1] * fac[3])
    load(2).wait()
    load(3).wait()

    def crop_rows(ri, one, other):
        got = dot(rows_of[...], jnp.concatenate([frame[ri, one], frame[ri, other]], 1)).astype(bf)
        for p in range(slots):
            cropped[ri, p, :, one * N : (one + 1) * N] = got[p * N : (p + 1) * N, :N]
            cropped[ri, p, :, other * N : (other + 1) * N] = got[p * N : (p + 1) * N, N:]

    def patch_copy(p, s, ri):
        return pltpu.make_async_remote_copy(
            src_ref=patch.at[p, ri], dst_ref=screens.at[s, ri],
            send_sem=p_send.at[p, ri], recv_sem=p_recv.at[s, ri], device_id=(2 * p + core, t), device_id_type=MESH)

    for ri in range(2):
        @pl.when(has_up)
        def _():
            halo_down(ri).wait_recv()

        sideways(ri, 0)

        @pl.when(has_down)
        def _():
            halo_up(ri).wait_recv()

        sideways(ri, 1)

    for ri in range(2):
        crop_rows(ri, 1, 2)

    for ri in range(2):
        for k in (2, 0, 1):
            @pl.when(has_left)
            def _():
                halo_right(ri, k).wait_recv()

            @pl.when(has_right)
            def _():
                halo_left(ri, k).wait_recv()

        crop_rows(ri, 0, 3)
        for p in range(slots):
            patch[p, ri] = dot(cropped[ri, p], cols_of[p]).astype(bf)

            @pl.when(y != 2 * p + core)
            def _():
                patch_copy(p, y, ri).start()

            @pl.when(y == 2 * p + core)
            def _():
                screens[y, ri] = patch[p, ri]

    mine = lax.div(y, 2)

    def grad_copy(s, p):
        return pltpu.make_async_remote_copy(
            src_ref=gout.at[s], dst_ref=gin.at[p],
            send_sem=g_send.at[s], recv_sem=g_recv.at[p], device_id=(s, t), device_id_type=MESH)

    @pl.when(lax.rem(y, 2) == core)
    def _():
        def screen(s):
            return (screens[s, 0].astype(f32) + 1.0) * fac[0], screens[s, 1].astype(f32) * fac[0]

        def arrive(s):
            @pl.when(y != s)
            def _():
                for ri in range(2):
                    patch_copy(0, s, ri).wait_recv()

        def forward(s, carry):
            arrive(s)
            sr, si = screen(s)
            xs = [mul_columns(wave[s, q], sr, si) for q in range(pairs)]
            xs = propagate(tab, xs, prop[0], prop[1])
            for q in range(pairs):
                wave[s + 1, q] = xs[q]
            return carry

        lax.fori_loop(0, depth - 1, forward, 0)
        arrive(depth - 1)
        sr, si = screen(depth - 1)
        xs = [mul_columns(wave[depth - 1, q], sr, si) for q in range(pairs)]
        xs = [swap(left(tab, 0, x)) for x in xs]
        xs = [mul_rows(right(tab, 1, x), prop[2], prop[3]) for x in xs]
        intensity = jnp.zeros((N, N), f32)
        for x in xs:
            for part in blocks(x):
                intensity = intensity + part * part
        valid = jnp.where(mine < counts[0], 4.0, 0.0)
        weight = (intensity - measured[mine]) * valid
        xs = [mul_rows(x, prop[4] * weight, -prop[5] * weight) for x in xs]
        xs = [swap(right(tab, 0, x)) for x in xs]
        us = [left(tab, 1, x) for x in xs]

        def leave(s, us):
            gr = jnp.zeros((N, N), f32)
            gi = jnp.zeros((N, N), f32)
            for q in range(pairs):
                u, v = blocks(us[q]), blocks(wave[s, q])
                for k in range(2):
                    gr = gr + u[k] * v[k] + u[2 + k] * v[2 + k]
                    gi = gi + u[2 + k] * v[k] - u[k] * v[2 + k]
            back = fac[1] * fac[1]
            gout[s, 0] = (gr * back).astype(bf)
            gout[s, 1] = (gi * back).astype(bf)

            @pl.when(y != s)
            def _():
                grad_copy(s, mine).start()

            @pl.when(y == s)
            def _():
                gin[mine] = gout[s]

            sr, si = screen(s)
            for q in range(pairs):
                wave[depth, q] = mul_columns(us[q], sr, -si)

        leave(depth - 1, us)

        def backward(k, carry):
            s = depth - 2 - k
            xs = [wave[depth, q] for q in range(pairs)]
            leave(s, propagate(tab, xs, prop[0], -prop[1]))
            return carry

        lax.fori_loop(0, depth - 1, backward, 0)

    for p in range(slots):
        @pl.when(y != 2 * p + core)
        def _():
            grad_copy(0, p).wait_recv()

        got = dot(jnp.concatenate([gin[p, 0], gin[p, 1]], 0), cols_back[p]).astype(bf)
        for ri in range(2):
            for cb in range(4):
                at = (0, 2, 3, 1)[cb]
                gcols[ri, p * N : (p + 1) * N, at * N : (at + 1) * N] = got[ri * N : (ri + 1) * N, cb * N : (cb + 1) * N]

    def fold_left(ri, k):
        lo, hi = pieces[k]
        return pltpu.make_async_remote_copy(
            src_ref=hout.at[0, ri, lo:hi], dst_ref=hin.at[0, ri, lo:hi],
            send_sem=fh_send.at[0, ri, k], recv_sem=fh_recv.at[0, ri, k], device_id=(y, t - 1), device_id_type=MESH)

    def fold_right(ri, k):
        lo, hi = pieces[k]
        return pltpu.make_async_remote_copy(
            src_ref=hout.at[1, ri, lo:hi], dst_ref=hin.at[1, ri, lo:hi],
            send_sem=fh_send.at[1, ri, k], recv_sem=fh_recv.at[1, ri, k], device_id=(y, t + 1), device_id_type=MESH)

    def send_sides(ri, k):
        @pl.when(has_left)
        def _():
            fold_left(ri, k).start()

        @pl.when(has_right)
        def _():
            fold_right(ri, k).start()

    for ri in range(2):
        got = dot(rows_back[...], gcols[ri, :, : 2 * N]).astype(bf)
        hout[0, ri] = got[:, :N]
        hout[1, ri] = got[:, N:]
        send_sides(ri, 0)
        send_sides(ri, 1)
    for ri in range(2):
        send_sides(ri, 2)
    for ri in range(2):
        got = dot(rows_back[...], gcols[ri, :, 2 * N :])
        gframe[ri, 0] = got[:, :N]
        gframe[ri, 1] = got[:, N:]

    def fold_up(ri):
        return pltpu.make_async_remote_copy(
            src_ref=vout.at[0, ri], dst_ref=vin.at[0, ri],
            send_sem=fv_send.at[0, ri], recv_sem=fv_recv.at[0, ri], device_id=(y, t - TCOLS), device_id_type=MESH)

    def fold_down(ri):
        return pltpu.make_async_remote_copy(
            src_ref=vout.at[1, ri], dst_ref=vin.at[1, ri],
            send_sem=fv_send.at[1, ri], recv_sem=fv_recv.at[1, ri], device_id=(y, t + TCOLS), device_id_type=MESH)

    def take_sides(ri, k):
        lo, hi = pieces[k]

        @pl.when(has_right)
        def _():
            fold_left(ri, k).wait_recv()
            gframe[ri, 1, lo:hi] = gframe[ri, 1, lo:hi] + hin[0, ri, lo:hi].astype(f32)

        @pl.when(has_left)
        def _():
            fold_right(ri, k).wait_recv()
            gframe[ri, 0, lo:hi] = gframe[ri, 0, lo:hi] + hin[1, ri, lo:hi].astype(f32)

    for ri in range(2):
        take_sides(ri, 0)
        vout[0, ri] = gframe[ri, :, 0:N].astype(bf)

        @pl.when(has_up)
        def _():
            fold_up(ri).start()

        take_sides(ri, 1)
        vout[1, ri] = gframe[ri, :, 3 * N : 4 * N].astype(bf)

        @pl.when(has_down)
        def _():
            fold_down(ri).start()

    for ri in range(2):
        take_sides(ri, 2)
        for cb in range(2):
            out[ri, :, cb * N : (cb + 1) * N] = gframe[ri, cb, N : 3 * N]

    for ri in range(2):
        @pl.when(has_up)
        def _():
            fold_down(ri).wait_recv()
            for cb in range(2):
                at = (ri, slice(0, N), slice(cb * N, (cb + 1) * N))
                out[at] = out[at] + vin[1, ri, cb].astype(f32)

        @pl.when(has_down)
        def _():
            fold_up(ri).wait_recv()
            for cb in range(2):
                at = (ri, slice(N, 2 * N), slice(cb * N, (cb + 1) * N))
                out[at] = out[at] + vin[0, ri, cb].astype(f32)

    for ri in range(2):
        @pl.when(has_down)
        def _():
            halo_down(ri).wait_send()
            fold_down(ri).wait_send()

        @pl.when(has_up)
        def _():
            halo_up(ri).wait_send()
            fold_up(ri).wait_send()

        @pl.when(has_right)
        def _():
            for k in range(3):
                halo_right(ri, k).wait_send()
                fold_right(ri, k).wait_send()

        @pl.when(has_left)
        def _():
            for k in range(3):
                halo_left(ri, k).wait_send()
                fold_left(ri, k).wait_send()

        for p in range(slots):
            @pl.when(y != 2 * p + core)
            def _():
                patch_copy(p, 0, ri).wait_send()

    for s in range(depth):
        @pl.when(jnp.logical_and(lax.rem(y, 2) == core, y != s))
        def _():
            grad_copy(s, 0).wait_send()


def body(depth, tiles, transmission, probe_modes, propagator_phase, measured, counts, offsets):
    slots = offsets.shape[1]
    pairs = probe_modes.shape[0] // 2
    bf, f32 = jnp.bfloat16, jnp.float32
    vmem = pl.BlockSpec(memory_space=pltpu.VMEM)
    hbm = pl.BlockSpec(memory_space=pl.ANY)
    smem = pl.BlockSpec(memory_space=pltpu.SMEM)
    dma = pltpu.SemaphoreType.DMA
    grad = pl.pallas_call(
        functools.partial(kernel, depth, tiles, slots, pairs),
        out_shape=jax.ShapeDtypeStruct((2, 2 * N, 2 * N), f32),
        in_specs=[hbm, hbm, hbm, hbm, smem, smem, hbm, hbm],
        out_specs=vmem,
        scratch_shapes=[
            pltpu.VMEM((2, 2 * N, 2 * N), f32),
            pltpu.VMEM(probe_modes.shape, f32),
            pltpu.VMEM((N, N), f32),
            pltpu.VMEM((slots, N, N), f32),
            pltpu.VMEM(TABLES.shape, bf),
            pltpu.VMEM(FACTORS.shape, f32),
            pltpu.VMEM((2, 4, 4 * N, N), bf),
            pltpu.VMEM((slots * N, 4 * N), bf),
            pltpu.VMEM((slots, 4 * N, N), bf),
            pltpu.VMEM((4 * N, slots * N), bf),
            pltpu.VMEM((slots, N, 4 * N), bf),
            pltpu.VMEM((2, slots, N, 4 * N), bf),
            pltpu.VMEM((slots, 2, N, N), bf),
            pltpu.VMEM((depth, 2, N, N), bf),
            pltpu.VMEM((depth + 1, pairs, 2 * N, 2 * N), f32),
            pltpu.VMEM((6, N, N), f32),
            pltpu.VMEM((depth, 2, N, N), bf),
            pltpu.VMEM((slots, 2, N, N), bf),
            pltpu.VMEM((2, slots * N, 4 * N), bf),
            pltpu.VMEM((2, 2, 4 * N, N), f32),
            pltpu.VMEM((2, 2, 4 * N, N), bf),
            pltpu.VMEM((2, 2, 4 * N, N), bf),
            pltpu.VMEM((2, 2, 2, N, N), bf),
            pltpu.VMEM((2, 2, 2, N, N), bf),
            dma((2, 2)), dma((5,)),
            dma((2, 2)), dma((2, 2)), dma((2, 2, 3)), dma((2, 2, 3)),
            dma((slots, 2)), dma((depth, 2)), dma((depth,)), dma((slots,)),
            dma((2, 2, 3)), dma((2, 2, 3)), dma((2, 2)), dma((2, 2)),
        ],
        compiler_params=pltpu.CompilerParams(
            collective_id=0, has_side_effects=True, vmem_limit_bytes=56 * 2**20
        ),
        cost_estimate=pl.CostEstimate(flops=2 * 10**10, bytes_accessed=3 * 2**20, transcendentals=2 * N * N),
    )(
        transmission[0, 0], probe_modes, propagator_phase, measured[0], counts, jnp.transpose(offsets[0]),
        jnp.asarray(TABLES), jnp.asarray(FACTORS),
    )
    return grad[None, None]


def solution(mesh):
    return jax.shard_map(
        functools.partial(body, mesh.shape["depth"], mesh.shape["tile"]),
        mesh=mesh,
        in_specs=(
            P("depth", "tile", None, None, None),
            P(),
            P(),
            P("tile", None, None, None),
            P("tile"),
            P("tile", None, None),
        ),
        out_specs=P("depth", "tile", None, None, None),
        check_vma=False,
    )
```

time: 74.4 us -> 65.5 us (0.88)
  local copies, waits for them, and re-layouts: 6.56 us -> 1.87 us
  Pallas kernels: 66.3 us -> 62.6 us
    unnamed x14 -> x1, local copies, waits for them, and re-layouts: 6.47 us -> 1.87 us
    pallas_call x1, Pallas kernels: 66.3 us -> 62.6 us  [body(): pl.pallas_call(functools.partial(kernel, depth, tiles, slots, pairs), out...]
where the time goes in v2:
time: 65.5 us; the launch traced here: 65.1 us
  Pallas kernels  62.6 us (96%)
  local copies, waits for them, and re-layouts  1.87 us (3%)
  between operations  0.66 us (1%)
    pallas_call x1, Pallas kernels, body(): pl.pallas_call(functools.partial(kernel, depth, tiles, slots, pairs), out...  62.6 us
    unnamed x1, local copies, waits for them, and re-layouts  1.87 us

profile of v2, /device:TPU:7, one launch (start us, length us, event | category | flops | bytes accessed | tf_op | source)
XLA Modules:
  0.0 65.1 jit_solution(11110737769352396972)
XLA Ops:
  0.7 62.6 %shard_map.82 = f32[2,256,256]{2,1,0:T(8,128)} custom-call(f32[2,256,256]{2,1,0:T(8,128)} %bitcast.7, f32[4,2,128,128]{3,2,1,0:T(8,128)} %probe_hbm.1, f32[128,128]{1,0:T(8,128)} %phase_hbm.1, f32[4,128,128]{2,1,0:T(8,128)} %bitcast.8, s32[1]{0:T(128)S(6)} %copy.10.counts, s32[2,4]{1,0:T(2,128)} %bitcast.9, bf16[2,256,256]{2,1,0:T(8,128)(2,1)} %constant.4.clone.tab_hbm, ...), custom_call_target="tpu_custom_call" | custom-call | flops 20000000000 | bytes 3145728 | tf_op jit(solution)/shard_map/pallas_call | solution.py:501
  63.2 1.9 %copy.11 = f32[1,1,2,256,256]{4,3,2,1,0:T(8,128)} copy(f32[1,1,2,256,256]{4,3,2,1,0:T(8,128)} %bitcast.6) | data formatting | bytes 1048576

commit v3 on v2

--- a/solution.py
+++ b/solution.py
@@ -12,6 +12,7 @@
 
 TCOLS = 4
 N = 128
+WORKERS = ((0, 1, 3, 6), (1, 2, 5, 7))
 MESH = pl.DeviceIdType.MESH
 CLASS_SCALES = 1.2742026, 1.2925407, 1.5548331, 1.5449858, 1.3945649, 1.3043629, 1.3043644, 1.3043595
 
@@ -53,11 +54,13 @@
 
 
 def left(tab, which, x):
-    return dot(tab[which], x.astype(jnp.bfloat16))
+    x = x.astype(jnp.bfloat16)
+    return jnp.concatenate([dot(tab[which, :N], x), dot(tab[which, N:], x)], 0)
 
 
 def right(tab, which, x):
-    return dot(x.astype(jnp.bfloat16), tab[which])
+    x = x.astype(jnp.bfloat16)
+    return jnp.concatenate([dot(x[:N], tab[which]), dot(x[N:], tab[which])], 0)
 
 
 def mul_columns(x, sr, si):
@@ -97,6 +100,9 @@
     bf = jnp.bfloat16
     f32 = jnp.float32
 
+    def worker(p):
+        return WORKERS[0][p] + core * (WORKERS[1][p] - WORKERS[0][p])
+
     def load_own(ri, half):
         part = (ri, slice(half * N, (half + 1) * N))
         return pltpu.make_async_copy(own_hbm.at[part], own.at[part], own_sem.at[ri, half])
@@ -190,7 +196,7 @@
         def _():
             halo_left(ri, k).start()
 
-    for ri in range(2):
+    def send_halo(ri):
         @pl.when(has_down)
         def _():
             halo_down(ri).start()
@@ -199,8 +205,9 @@
         def _():
             halo_up(ri).start()
 
-    for ri in range(2):
         sideways(ri, 2)
+
+    send_halo(0)
 
     for p in range(slots):
         r, c = offsets[0, p], offsets[1, p]
@@ -236,9 +243,9 @@
     def patch_copy(p, s, ri):
         return pltpu.make_async_remote_copy(
             src_ref=patch.at[p, ri], dst_ref=screens.at[s, ri],
-            send_sem=p_send.at[p, ri], recv_sem=p_recv.at[s, ri], device_id=(2 * p + core, t), device_id_type=MESH)
-
-    for ri in range(2):
+            send_sem=p_send.at[p, ri], recv_sem=p_recv.at[s, ri], device_id=(worker(p), t), device_id_type=MESH)
+
+    def take_rows(ri):
         @pl.when(has_up)
         def _():
             halo_down(ri).wait_recv()
@@ -251,10 +258,12 @@
 
         sideways(ri, 1)
 
-    for ri in range(2):
+    take_rows(0)
+    send_halo(1)
+    for ri in range(2):
+        if ri == 1:
+            take_rows(1)
         crop_rows(ri, 1, 2)
-
-    for ri in range(2):
         for k in (2, 0, 1):
             @pl.when(has_left)
             def _():
@@ -268,22 +277,24 @@
         for p in range(slots):
             patch[p, ri] = dot(cropped[ri, p], cols_of[p]).astype(bf)
 
-            @pl.when(y != 2 * p + core)
+        for p in range(slots):
+            @pl.when(y != worker(p))
             def _():
                 patch_copy(p, y, ri).start()
 
-            @pl.when(y == 2 * p + core)
+            @pl.when(y == worker(p))
             def _():
                 screens[y, ri] = patch[p, ri]
 
-    mine = lax.div(y, 2)
-
-    def grad_copy(s, p):
-        return pltpu.make_async_remote_copy(
-            src_ref=gout.at[s], dst_ref=gin.at[p],
-            send_sem=g_send.at[s], recv_sem=g_recv.at[p], device_id=(s, t), device_id_type=MESH)
-
-    @pl.when(lax.rem(y, 2) == core)
+    mine = sum(p * (y == worker(p)).astype(jnp.int32) for p in range(slots))
+    working = sum((y == worker(p)).astype(jnp.int32) for p in range(slots)) > 0
+
+    def grad_copy(s, p, ri):
+        return pltpu.make_async_remote_copy(
+            src_ref=gout.at[s, ri], dst_ref=gin.at[p, ri],
+            send_sem=g_send.at[s, ri], recv_sem=g_recv.at[p, ri], device_id=(s, t), device_id_type=MESH)
+
+    @pl.when(working)
     def _():
         def screen(s):
             return (screens[s, 0].astype(f32) + 1.0) * fac[0], screens[s, 1].astype(f32) * fac[0]
@@ -319,7 +330,10 @@
         xs = [swap(right(tab, 0, x)) for x in xs]
         us = [left(tab, 1, x) for x in xs]
 
-        def leave(s, us):
+        for q in range(pairs):
+            wave[depth, q] = us[q]
+
+        def gradient(s, us):
             gr = jnp.zeros((N, N), f32)
             gi = jnp.zeros((N, N), f32)
             for q in range(pairs):
@@ -331,69 +345,68 @@
             gout[s, 0] = (gr * back).astype(bf)
             gout[s, 1] = (gi * back).astype(bf)
 
+        def leave(s):
             @pl.when(y != s)
             def _():
-                grad_copy(s, mine).start()
+                for ri in range(2):
+                    grad_copy(s, mine, ri).start()
 
             @pl.when(y == s)
             def _():
                 gin[mine] = gout[s]
 
+        def backward(k, carry):
+            s = depth - 1 - k
+            us = [wave[depth, q] for q in range(pairs)]
             sr, si = screen(s)
+            xs = propagate(tab, [mul_columns(u, sr, -si) for u in us], prop[0], -prop[1])
+            gradient(s, us)
             for q in range(pairs):
-                wave[depth, q] = mul_columns(us[q], sr, -si)
-
-        leave(depth - 1, us)
-
-        def backward(k, carry):
-            s = depth - 2 - k
-            xs = [wave[depth, q] for q in range(pairs)]
-            leave(s, propagate(tab, xs, prop[0], -prop[1]))
+                wave[depth, q] = xs[q]
+            leave(s)
             return carry
 
         lax.fori_loop(0, depth - 1, backward, 0)
-
-    for p in range(slots):
-        @pl.when(y != 2 * p + core)
-        def _():
-            grad_copy(0, p).wait_recv()
-
-        got = dot(jnp.concatenate([gin[p, 0], gin[p, 1]], 0), cols_back[p]).astype(bf)
-        for ri in range(2):
+        gradient(0, [wave[depth, q] for q in range(pairs)])
+        leave(0)
+
+    def fold_left(ri, k):
+        lo, hi = pieces[k]
+        return pltpu.make_async_remote_copy(
+            src_ref=hout.at[0, ri, lo:hi], dst_ref=hin.at[0, ri, lo:hi],
+            send_sem=fh_send.at[0, ri, k], recv_sem=fh_recv.at[0, ri, k], device_id=(y, t - 1), device_id_type=MESH)
+
+    def fold_right(ri, k):
+        lo, hi = pieces[k]
+        return pltpu.make_async_remote_copy(
+            src_ref=hout.at[1, ri, lo:hi], dst_ref=hin.at[1, ri, lo:hi],
+            send_sem=fh_send.at[1, ri, k], recv_sem=fh_recv.at[1, ri, k], device_id=(y, t + 1), device_id_type=MESH)
+
+    def send_sides(ri, k):
+        @pl.when(has_left)
+        def _():
+            fold_left(ri, k).start()
+
+        @pl.when(has_right)
+        def _():
+            fold_right(ri, k).start()
+
+    for ri in range(2):
+        for p in range(slots):
+            @pl.when(y != worker(p))
+            def _():
+                grad_copy(0, p, ri).wait_recv()
+
+        for p in range(slots):
+            got = dot(gin[p, ri], cols_back[p]).astype(bf)
             for cb in range(4):
                 at = (0, 2, 3, 1)[cb]
-                gcols[ri, p * N : (p + 1) * N, at * N : (at + 1) * N] = got[ri * N : (ri + 1) * N, cb * N : (cb + 1) * N]
-
-    def fold_left(ri, k):
-        lo, hi = pieces[k]
-        return pltpu.make_async_remote_copy(
-            src_ref=hout.at[0, ri, lo:hi], dst_ref=hin.at[0, ri, lo:hi],
-            send_sem=fh_send.at[0, ri, k], recv_sem=fh_recv.at[0, ri, k], device_id=(y, t - 1), device_id_type=MESH)
-
-    def fold_right(ri, k):
-        lo, hi = pieces[k]
-        return pltpu.make_async_remote_copy(
-            src_ref=hout.at[1, ri, lo:hi], dst_ref=hin.at[1, ri, lo:hi],
-            send_sem=fh_send.at[1, ri, k], recv_sem=fh_recv.at[1, ri, k], device_id=(y, t + 1), device_id_type=MESH)
-
-    def send_sides(ri, k):
-        @pl.when(has_left)
-        def _():
-            fold_left(ri, k).start()
-
-        @pl.when(has_right)
-        def _():
-            fold_right(ri, k).start()
-
-    for ri in range(2):
+                gcols[ri, p * N : (p + 1) * N, at * N : (at + 1) * N] = got[:, cb * N : (cb + 1) * N]
         got = dot(rows_back[...], gcols[ri, :, : 2 * N]).astype(bf)
         hout[0, ri] = got[:, :N]
         hout[1, ri] = got[:, N:]
         send_sides(ri, 0)
         send_sides(ri, 1)
-    for ri in range(2):
-        send_sides(ri, 2)
-    for ri in range(2):
         got = dot(rows_back[...], gcols[ri, :, 2 * N :])
         gframe[ri, 0] = got[:, :N]
         gframe[ri, 1] = got[:, N:]
@@ -435,6 +448,8 @@
         @pl.when(has_down)
         def _():
             fold_down(ri).start()
+
+        send_sides(ri, 2)
 
     for ri in range(2):
         take_sides(ri, 2)
@@ -480,14 +495,15 @@
                 fold_left(ri, k).wait_send()
 
         for p in range(slots):
-            @pl.when(y != 2 * p + core)
+            @pl.when(y != worker(p))
             def _():
                 patch_copy(p, 0, ri).wait_send()
 
     for s in range(depth):
-        @pl.when(jnp.logical_and(lax.rem(y, 2) == core, y != s))
-        def _():
-            grad_copy(s, 0).wait_send()
+        @pl.when(jnp.logical_and(working, y != s))
+        def _():
+            for ri in range(2):
+                grad_copy(s, 0, ri).wait_send()
 
 
 def body(depth, tiles, transmission, probe_modes, propagator_phase, measured, counts, offsets):
@@ -500,7 +516,7 @@
     dma = pltpu.SemaphoreType.DMA
     grad = pl.pallas_call(
         functools.partial(kernel, depth, tiles, slots, pairs),
-        out_shape=jax.ShapeDtypeStruct((2, 2 * N, 2 * N), f32),
+        out_shape=pltpu.VMEM((2, 2 * N, 2 * N), f32),
         in_specs=[hbm, hbm, hbm, hbm, smem, smem, hbm, hbm],
         out_specs=vmem,
         scratch_shapes=[
@@ -530,7 +546,7 @@
             pltpu.VMEM((2, 2, 2, N, N), bf),
             dma((2, 2)), dma((5,)),
             dma((2, 2)), dma((2, 2)), dma((2, 2, 3)), dma((2, 2, 3)),
-            dma((slots, 2)), dma((depth, 2)), dma((depth,)), dma((slots,)),
+            dma((slots, 2)), dma((depth, 2)), dma((depth, 2)), dma((slots, 2)),
             dma((2, 2, 3)), dma((2, 2, 3)), dma((2, 2)), dma((2, 2)),
         ],
         compiler_params=pltpu.CompilerParams(

time: 65.5 us -> 64.3 us (0.982)
  local copies, waits for them, and re-layouts: 1.87 us -> 0.8 us
    unnamed x1, local copies, waits for them, and re-layouts: 1.87 us -> 0.8 us
where the time goes in v3:
time: 64.3 us; the launch traced here: 64 us
  Pallas kernels  62.5 us (97%)
  local copies, waits for them, and re-layouts  0.8 us (1%)
  between operations  0.66 us (1%)
    pallas_call x1, Pallas kernels, body(): pl.pallas_call(functools.partial(kernel, depth, tiles, slots, pairs), out...  62.5 us

profile of v3, /device:TPU:7, one launch (start us, length us, event | category | flops | bytes accessed | tf_op | source)
XLA Modules:
  0.0 64.0 jit_solution(11054428143685075959)
XLA Ops:
  0.7 62.5 %shard_map.82 = f32[2,256,256]{2,1,0:T(8,128)S(1)} custom-call(f32[2,256,256]{2,1,0:T(8,128)} %bitcast.7, f32[4,2,128,128]{3,2,1,0:T(8,128)} %probe_hbm.1, f32[128,128]{1,0:T(8,128)} %phase_hbm.1, f32[4,128,128]{2,1,0:T(8,128)} %bitcast.8, s32[1]{0:T(128)S(6)} %copy.11.counts, s32[2,4]{1,0:T(2,128)} %bitcast.9, bf16[2,256,256]{2,1,0:T(8,128)(2,1)} %constant.4.clone.tab_hbm, ...), custom_call_target="tpu_custom_call" | custom-call | flops 20000000000 | bytes 3145728 | tf_op jit(solution)/shard_map/pallas_call | solution.py:517
  63.2 0.8 %copy.10 = f32[1,1,2,256,256]{4,3,2,1,0:T(8,128)} copy(f32[1,1,2,256,256]{4,3,2,1,0:T(8,128)S(1)} %bitcast.6) | data formatting | bytes 1048576

commit v4 on v3

--- a/solution.py
+++ b/solution.py
@@ -87,7 +87,7 @@
     own, probe, phase, measured, tab, fac,
     frame, rows_of, cols_of, rows_back, cols_back, cropped, patch, screens, wave, prop, gout, gin, gcols, gframe,
     hout, hin, vout, vin,
-    own_sem, in_sem,
+    own_sem, in_sem, ring_sem,
     v_send, v_recv, h_send, h_recv, p_send, p_recv, g_send, g_recv, fh_send, fh_recv, fv_send, fv_recv,
 ):
     y = lax.axis_index("depth")
@@ -121,8 +121,9 @@
         @pl.when(there)
         def _():
             pl.semaphore_signal(barrier, inc=1, device_id=(y, t + by), device_id_type=MESH)
-    for k in range(1, depth):
-        pl.semaphore_signal(barrier, inc=1, device_id=(lax.rem(y + k, depth), t), device_id_type=MESH)
+    both_ways = (lax.rem(y + 1, depth), lax.rem(y + depth - 1, depth))
+    for beside in both_ways:
+        pl.semaphore_signal(barrier, inc=1, device_id=(beside, t), device_id_type=MESH)
 
     for k in range(5):
         load(k).start()
@@ -160,8 +161,17 @@
 
     pl.semaphore_wait(
         barrier,
-        depth - 1 + sum(there.astype(jnp.int32) for there, _ in around),
+        2 + sum(there.astype(jnp.int32) for there, _ in around),
     )
+
+    rounds = depth // 2 - 1
+
+    def hear_further(k):
+        if 0 < k <= rounds:
+            pl.semaphore_wait(ring_sem.at[k - 1], 2)
+        if k < rounds:
+            for beside in both_ways:
+                pl.semaphore_signal(ring_sem.at[k], inc=1, device_id=(beside, t), device_id_type=MESH)
 
     def halo_down(ri):
         return pltpu.make_async_remote_copy(
@@ -208,6 +218,7 @@
         sideways(ri, 2)
 
     send_halo(0)
+    hear_further(0)
 
     for p in range(slots):
         r, c = offsets[0, p], offsets[1, p]
@@ -233,6 +244,7 @@
         wave[0, q] = square(one[0] * fac[3], two[0] * fac[3], one[1] * fac[3], two[1] * fac[3])
     load(2).wait()
     load(3).wait()
+    hear_further(1)
 
     def crop_rows(ri, one, other):
         got = dot(rows_of[...], jnp.concatenate([frame[ri, one], frame[ri, other]], 1)).astype(bf)
@@ -260,10 +272,13 @@
 
     take_rows(0)
     send_halo(1)
+    hear_further(2)
     for ri in range(2):
         if ri == 1:
             take_rows(1)
         crop_rows(ri, 1, 2)
+        if ri == 0:
+            hear_further(3)
         for k in (2, 0, 1):
             @pl.when(has_left)
             def _():
@@ -544,7 +559,7 @@
             pltpu.VMEM((2, 2, 4 * N, N), bf),
             pltpu.VMEM((2, 2, 2, N, N), bf),
             pltpu.VMEM((2, 2, 2, N, N), bf),
-            dma((2, 2)), dma((5,)),
+            dma((2, 2)), dma((5,)), pltpu.SemaphoreType.REGULAR((max(1, depth // 2 - 1),)),
             dma((2, 2)), dma((2, 2)), dma((2, 2, 3)), dma((2, 2, 3)),
             dma((slots, 2)), dma((depth, 2)), dma((depth, 2)), dma((slots, 2)),
             dma((2, 2, 3)), dma((2, 2, 3)), dma((2, 2)), dma((2, 2)),

time: 64.3 us -> 61.7 us (0.960)
  Pallas kernels: 62.5 us -> 60.1 us
    pallas_call x1, Pallas kernels: 62.5 us -> 60.1 us  [body(): pl.pallas_call(functools.partial(kernel, depth, tiles, slots, pairs), out...]
where the time goes in v4:
time: 61.7 us; the launch traced here: 61.6 us
  Pallas kernels  60.1 us (97%)
  local copies, waits for them, and re-layouts  0.8 us (1%)
  between operations  0.66 us (1%)
    pallas_call x1, Pallas kernels, body(): pl.pallas_call(functools.partial(kernel, depth, tiles, slots, pairs), out...  60.1 us

profile of v4, /device:TPU:7, one launch (start us, length us, event | category | flops | bytes accessed | tf_op | source)
XLA Modules:
  0.0 61.6 jit_solution(6237383350765321294)
XLA Ops:
  0.7 60.1 %shard_map.82 = f32[2,256,256]{2,1,0:T(8,128)S(1)} custom-call(f32[2,256,256]{2,1,0:T(8,128)} %bitcast.7, f32[4,2,128,128]{3,2,1,0:T(8,128)} %probe_hbm.1, f32[128,128]{1,0:T(8,128)} %phase_hbm.1, f32[4,128,128]{2,1,0:T(8,128)} %bitcast.8, s32[1]{0:T(128)S(6)} %copy.11.counts, s32[2,4]{1,0:T(2,128)} %bitcast.9, bf16[2,256,256]{2,1,0:T(8,128)(2,1)} %constant.4.clone.tab_hbm, ...), custom_call_target="tpu_custom_call" | custom-call | flops 20000000000 | bytes 3145728 | tf_op jit(solution)/shard_map/pallas_call | solution.py:532
  60.8 0.8 %copy.10 = f32[1,1,2,256,256]{4,3,2,1,0:T(8,128)} copy(f32[1,1,2,256,256]{4,3,2,1,0:T(8,128)S(1)} %bitcast.6) | data formatting | bytes 1048576

commit v5 on v4

--- a/solution.py
+++ b/solution.py
@@ -152,12 +152,14 @@
         for ri in range(2):
             frame[ri, 3] = outside(ri, (4 * N, N))
 
-    for ri in range(2):
+    def fill(ri):
         for half in range(2):
             load_own(ri, half).wait()
             for cb in range(2):
                 got = own[ri, half * N : (half + 1) * N, cb * N : (cb + 1) * N]
                 frame[ri, 1 + cb, (1 + half) * N : (2 + half) * N] = (got - 1.0 if ri == 0 else got).astype(bf)
+
+    fill(0)
 
     pl.semaphore_wait(
         barrier,
@@ -219,6 +221,7 @@
 
     send_halo(0)
     hear_further(0)
+    fill(1)
 
     for p in range(slots):
         r, c = offsets[0, p], offsets[1, p]
@@ -413,15 +416,15 @@
                 grad_copy(0, p, ri).wait_recv()
 
         for p in range(slots):
-            got = dot(gin[p, ri], cols_back[p]).astype(bf)
-            for cb in range(4):
-                at = (0, 2, 3, 1)[cb]
-                gcols[ri, p * N : (p + 1) * N, at * N : (at + 1) * N] = got[:, cb * N : (cb + 1) * N]
+            sides = jnp.concatenate([cols_back[p, :, :N], cols_back[p, :, 3 * N :]], 1)
+            gcols[ri, p * N : (p + 1) * N, : 2 * N] = dot(gin[p, ri], sides).astype(bf)
         got = dot(rows_back[...], gcols[ri, :, : 2 * N]).astype(bf)
         hout[0, ri] = got[:, :N]
         hout[1, ri] = got[:, N:]
         send_sides(ri, 0)
         send_sides(ri, 1)
+        for p in range(slots):
+            gcols[ri, p * N : (p + 1) * N, 2 * N :] = dot(gin[p, ri], cols_back[p, :, N : 3 * N]).astype(bf)
         got = dot(rows_back[...], gcols[ri, :, 2 * N :])
         gframe[ri, 0] = got[:, :N]
         gframe[ri, 1] = got[:, N:]

time: 61.7 us -> 61.6 us (level)
  no operation moved by 1% of the time
where the time goes in v5:
time: 61.6 us; the launch traced here: 61.5 us
  Pallas kernels  60 us (97%)
  local copies, waits for them, and re-layouts  0.8 us (1%)
  between operations  0.66 us (1%)
    pallas_call x1, Pallas kernels, body(): pl.pallas_call(functools.partial(kernel, depth, tiles, slots, pairs), out...  60 us

profile of v5, /device:TPU:7, one launch (start us, length us, event | category | flops | bytes accessed | tf_op | source)
XLA Modules:
  0.0 61.5 jit_solution(15015182753426545691)
XLA Ops:
  0.7 60.0 %shard_map.82 = f32[2,256,256]{2,1,0:T(8,128)S(1)} custom-call(f32[2,256,256]{2,1,0:T(8,128)} %bitcast.7, f32[4,2,128,128]{3,2,1,0:T(8,128)} %probe_hbm.1, f32[128,128]{1,0:T(8,128)} %phase_hbm.1, f32[4,128,128]{2,1,0:T(8,128)} %bitcast.8, s32[1]{0:T(128)S(6)} %copy.11.counts, s32[2,4]{1,0:T(2,128)} %bitcast.9, bf16[2,256,256]{2,1,0:T(8,128)(2,1)} %constant.4.clone.tab_hbm, ...), custom_call_target="tpu_custom_call" | custom-call | flops 20000000000 | bytes 3145728 | tf_op jit(solution)/shard_map/pallas_call | solution.py:535
  60.7 0.8 %copy.10 = f32[1,1,2,256,256]{4,3,2,1,0:T(8,128)} copy(f32[1,1,2,256,256]{4,3,2,1,0:T(8,128)S(1)} %bitcast.6) | data formatting | bytes 1048576
